TPU v7x, 512 devices: a whole 4x4x16 slice. The times are simulated.
512 devices in a mesh: ex: 32 (over y, x, core), fac: 16 (over z).
Axes of the slice: x: 4, y: 4, z: 16, core: 2. Of those that a mesh axis runs over, the one named last changes fastest.
Arguments:
- samples: bfloat16 [32768, 1024], P('ex'), may hold values from -6 to 6
- counts: int32 [32], P('ex'), may hold values from 256 to 1024, as said below
- panel_weight: bfloat16 [1024, 1024], P(None, 'fac'), may hold values from -0.1875 to 0.1875
- rest_weight: bfloat16 [1024, 11264], P(None, 'fac'), may hold values from -0.1875 to 0.1875
Outputs:
- panel_factor: float32 [1024, 1024], P('fac')
- rest_factor: float32 [11264, 1024], P(('fac', 'ex'))
Inputs may be any that keep to these rules, and one draw needn't show every extreme that they name: `counts`: live examples of a slab; some slab is full in every draw.
All inputs are finite; a program needn't handle non-finite values.
Results may differ from a plain program's by a relative error of at most 0.018.
Values may be sent and summed in bfloat16 or wider, within the bound.
A program may use at most 64 MiB of HBM per device.

v0:
```python
import jax
import jax.numpy as jnp
from jax import lax
from jax.sharding import PartitionSpec as P


def on_device(samples, counts, panel_weight, rest_weight):
    rows = samples.shape[0]
    total = rows * lax.axis_size("ex")
    live = (jnp.arange(rows, dtype=jnp.int32) < counts[0])[:, None]
    own_width = panel_weight.shape[1]

    def features_of(weight):
        return jnp.where(
            live, jax.nn.relu(jnp.dot(samples, weight, preferred_element_type=jnp.float32)), 0.0
        ).astype(jnp.bfloat16)

    own_panel = features_of(panel_weight)
    panel_feats = lax.all_gather(own_panel, "fac", axis=1, tiled=True)
    rest_feats = features_of(rest_weight)
    dims = (((0,), (0,)), ((), ()))
    panel_part = lax.dot_general(own_panel, panel_feats, dims, preferred_element_type=jnp.float32)
    share = rest_feats.shape[1] // lax.axis_size("ex")
    rest_part = lax.dot_general(rest_feats, panel_feats, dims, preferred_element_type=jnp.float32)
    panel_sum, rest_sum = lax.psum((panel_part, rest_part), "ex")
    rest_rows = lax.dynamic_slice_in_dim(rest_sum, lax.axis_index("ex") * share, share, 0)
    panel_rows = lax.all_gather(panel_sum, "fac", axis=0, tiled=True)
    panel_gram = panel_rows / total + jnp.eye(panel_rows.shape[0], dtype=jnp.float32)
    factor = jnp.linalg.cholesky(panel_gram)
    rest_gram = rest_rows / total
    rest_factor = lax.linalg.triangular_solve(
        factor, rest_gram, left_side=False, lower=True, transpose_a=True
    )
    panel_factor = lax.dynamic_slice_in_dim(factor, lax.axis_index("fac") * own_width, own_width, 0)
    return (panel_factor, rest_factor)


def solution(mesh):
    in_specs = (P("ex", None), P("ex"), P(None, "fac"), P(None, "fac"))
    out_specs = (P("fac", None), P(("fac", "ex"), None))
    return jax.shard_map(
        on_device, mesh=mesh, in_specs=in_specs, out_specs=out_specs, check_vma=False
    )
```

profile of v0, /device:TPU:6, one launch (start us, length us, event | category | flops | bytes accessed | tf_op | source)
XLA Modules:
  0.0 672.0 jit_solution(3456490553327815212)
XLA Ops:
  8.8 2.3 fusion.3
  11.2 77.6 %all-gather.3.cloned.1.call-done = bf16[1024,1024]{0,1:T(8,128)(2,1)} async-done(((bf16[1024,64]{0,1:T(8,128)(2,1)}), bf16[1024,1024]{0,1:T(8,128)(2,1)}) %all-gather.3.cloned.1.call-update) | async-done | bytes 2097168 | tf_op jit(solution)/shard_map/all_gather | solution.py:19
  88.8 3.1 fusion.67
  91.9 7.9 %fusion.9 = f32[704,1024]{1,0:T(8,128)} fusion(bf16[1024,1024]{0,1:T(8,128)(2,1)} %all-gather.3.cloned.1.call-done, bf16[1024,1024]{1,0:T(8,128)(2,1)S(1)} %copy-done, bf16[1024,704]{0,1:T(8,128)(2,1)S(1)} %copy-done.3, pred[1024]{0:T(1024)(128)(4,1)S(1)} %iota_compare_fusion.4), kind=kOutput, calls=%fused_computation.39 | convolution fusion | flops 2954952704 | bytes 8520704 | tf_op jit(solution)/shard_map/dot_general | solution.py:24
  99.8 138.5 %all-reduce.4.cloned.1.call-done = (f32[64,1024]{1,0:T(8,128)}, f32[704,1024]{1,0:T(8,128)}) async-done(((f32[64,1024]{1,0:T(8,128)}, f32[704,1024]{1,0:T(8,128)}), (f32[64,1024]{1,0:T(8,128)}, f32[704,1024]{1,0:T(8,128)})) %all-reduce.4.cloned.1.call-update) | async-done | bytes 3145744 | tf_op jit(solution)/shard_map/psum | solution.py:25
  239.4 78.9 %all-gather.5.cloned.1.call-done = f32[1024,1024]{1,0:T(8,128)} async-done(((f32[64,1024]{1,0:T(8,128)}), f32[1024,1024]{1,0:T(8,128)}) %all-gather.5.cloned.1.call-update) | async-done | bytes 4194320 | tf_op jit(solution)/shard_map/all_gather | solution.py:27
  318.3 5.3 copy.8
  323.6 5.0 convert_add_fusion
  328.6 5.8 copy.9
  334.4 4.5 fusion
  338.9 1.9 copy-done.1
  340.8 11.7 %cholesky.223 = f32[128,128]{1,0:T(8,128)S(1)} custom-call(f32[128,128]{1,0:T(8,128)S(1)} %cholesky.580), custom_call_target="Cholesky" | custom-call | tf_op jit(solution)/shard_map/jit(cholesky)/cholesky | solution.py:29
  352.6 9.8 %custom-call.62 = f32[1,128,128]{1,2,0:T(8,128)S(1)} custom-call(f32[1,128,128]{2,1,0:T(8,128)S(1)} %get-tuple-element.45), custom_call_target="InvertDiagBlocksLowerTriangular" | custom-call | tf_op jit(solution)/shard_map/jit(cholesky)/cholesky | solution.py:29
  362.4 2.5 cholesky.255
  364.9 2.3 constant_dynamic-update-slice_fusion.31
  367.2 1.5 convolution_subtract_fusion
  368.8 11.8 %cholesky.244 = f32[128,128]{1,0:T(8,128)S(1)} custom-call(f32[128,128]{1,0:T(8,128)S(1)} %cholesky.584), custom_call_target="Cholesky" | custom-call | tf_op jit(solution)/shard_map/jit(cholesky)/cholesky | solution.py:29
  381.3 9.8 %custom-call.63 = f32[1,128,128]{1,2,0:T(8,128)S(1)} custom-call(f32[1,128,128]{2,1,0:T(8,128)S(1)} %get-tuple-element.42), custom_call_target="InvertDiagBlocksLowerTriangular" | custom-call | tf_op jit(solution)/shard_map/jit(cholesky)/cholesky | solution.py:29
  392.4 2.1 convolution_subtract_fusion.1
  394.5 11.7 %cholesky.468 = f32[128,128]{1,0:T(8,128)S(1)} custom-call(f32[128,128]{1,0:T(8,128)S(1)} %cholesky.589), custom_call_target="Cholesky" | custom-call | tf_op jit(solution)/shard_map/jit(cholesky)/cholesky | solution.py:29
  407.5 9.8 %custom-call.64 = f32[1,128,128]{1,2,0:T(8,128)S(1)} custom-call(f32[1,128,128]{2,1,0:T(8,128)S(1)} %get-tuple-element.39), custom_call_target="InvertDiagBlocksLowerTriangular" | custom-call | tf_op jit(solution)/shard_map/jit(cholesky)/cholesky | solution.py:29
  418.5 2.3 convolution_subtract_fusion.2
  420.8 11.9 %cholesky.487 = f32[128,128]{1,0:T(8,128)S(1)} custom-call(f32[128,128]{1,0:T(8,128)S(1)} %cholesky.594), custom_call_target="Cholesky" | custom-call | tf_op jit(solution)/shard_map/jit(cholesky)/cholesky | solution.py:29
  434.0 9.8 %custom-call.65 = f32[1,128,128]{1,2,0:T(8,128)S(1)} custom-call(f32[1,128,128]{2,1,0:T(8,128)S(1)} %get-tuple-element.36), custom_call_target="InvertDiagBlocksLowerTriangular" | custom-call | tf_op jit(solution)/shard_map/jit(cholesky)/cholesky | solution.py:29
  445.0 2.3 convolution_subtract_fusion.3
  447.3 11.7 %cholesky.506 = f32[128,128]{1,0:T(8,128)S(1)} custom-call(f32[128,128]{1,0:T(8,128)S(1)} %cholesky.599), custom_call_target="Cholesky" | custom-call | tf_op jit(solution)/shard_map/jit(cholesky)/cholesky | solution.py:29
  460.4 10.3 %custom-call.66 = f32[1,128,128]{1,2,0:T(8,128)S(1)} custom-call(f32[1,128,128]{2,1,0:T(8,128)S(1)} %get-tuple-element.33), custom_call_target="InvertDiagBlocksLowerTriangular" | custom-call | tf_op jit(solution)/shard_map/jit(cholesky)/cholesky | solution.py:29
  471.7 2.3 convolution_subtract_fusion.4
  474.0 11.7 %cholesky.526 = f32[128,128]{1,0:T(8,128)S(1)} custom-call(f32[128,128]{1,0:T(8,128)S(1)} %cholesky.604), custom_call_target="Cholesky" | custom-call | tf_op jit(solution)/shard_map/jit(cholesky)/cholesky | solution.py:29
  487.0 9.8 %custom-call.67 = f32[1,128,128]{1,2,0:T(8,128)S(1)} custom-call(f32[1,128,128]{2,1,0:T(8,128)S(1)} %get-tuple-element.30), custom_call_target="InvertDiagBlocksLowerTriangular" | custom-call | tf_op jit(solution)/shard_map/jit(cholesky)/cholesky | solution.py:29
  497.7 2.0 convolution_subtract_fusion.5
  499.8 11.9 %cholesky.546 = f32[128,128]{1,0:T(8,128)S(1)} custom-call(f32[128,128]{1,0:T(8,128)S(1)} %cholesky.609), custom_call_target="Cholesky" | custom-call | tf_op jit(solution)/shard_map/jit(cholesky)/cholesky | solution.py:29
  512.9 9.8 %custom-call.68 = f32[1,128,128]{1,2,0:T(8,128)S(1)} custom-call(f32[1,128,128]{2,1,0:T(8,128)S(1)} %get-tuple-element.27), custom_call_target="InvertDiagBlocksLowerTriangular" | custom-call | tf_op jit(solution)/shard_map/jit(cholesky)/cholesky | solution.py:29
  523.5 1.8 convolution_subtract_fusion.6
  525.3 11.7 %cholesky.564 = f32[128,128]{1,0:T(8,128)S(1)} custom-call(f32[128,128]{1,0:T(8,128)S(1)} %convolution_subtract_fusion.6), custom_call_target="Cholesky" | custom-call | tf_op jit(solution)/shard_map/jit(cholesky)/cholesky | solution.py:29
  544.1 6.6 fusion.1
  550.6 23.2 %while.1 = (s32[]{:T(128)}, f32[1024,1024]{1,0:T(8,128)}, s32[8,2]{0,1:T(2,128)S(1)}, f32[8,128,128]{2,1,0:T(8,128)S(1)}, s32[]{:T(128)}) while((s32[]{:T(128)}, f32[1024,1024]{1,0:T(8,128)}, s32[8,2]{0,1:T(2,128)S(1)}, f32[8,128,128]{2,1,0:T(8,128)S(1)}, s32[]{:T(128)}) %tuple.62), condition=%wide.while_cond, body=%wide.while_body.sunk | while | flops 2 | bytes 131189 | solution.py:31
  551.2 2.3 bitcast_dynamic-update-slice_fusion.2
  554.1 2.3 bitcast_dynamic-update-slice_fusion.2
  557.1 2.3 bitcast_dynamic-update-slice_fusion.2
  560.0 2.3 bitcast_dynamic-update-slice_fusion.2
  562.9 2.3 bitcast_dynamic-update-slice_fusion.2
  565.8 2.3 bitcast_dynamic-update-slice_fusion.2
  568.7 2.3 bitcast_dynamic-update-slice_fusion.2
  571.6 2.2 bitcast_dynamic-update-slice_fusion.2
  573.8 78.6 %custom-call.69 = f32[8,128,128]{1,2,0:T(8,128)S(1)} custom-call(f32[8,128,128]{2,1,0:T(8,128)S(1)} %get-tuple-element.9), custom_call_target="InvertDiagBlocksLowerTriangular" | custom-call | tf_op jit(solution)/shard_map/triangular_solve | solution.py:31
  661.2 1.5 convolution_subtract_fusion.11
  662.8 1.7 constant_dynamic-slice_fusion.1
  (76 shorter events, 31.5 us)
Async XLA Ops:
  7.2 1.6 copy-start
  7.2 84.7 %copy-start.3 = (bf16[1024,704]{0,1:T(8,128)(2,1)S(1)}, bf16[1024,704]{0,1:T(8,128)(2,1)}, u32[]{:S(2)}) copy-start(bf16[1024,704]{0,1:T(8,128)(2,1)} %param.7) | copy-start | bytes 4325380
  7.2 81.6 %all-gather.3.cloned.1.call-start = ((), (), s32[]{:S(2)}) async-start(), calls=%async_computation | async-start | bytes 2228224 | tf_op jit(solution)/shard_map/all_gather | solution.py:19
  11.1 227.3 %all-reduce.4.cloned.1.call-start = ((), (), s32[]{:S(2)}) async-start(), calls=%async_computation.2 | async-start | bytes 6291456 | tf_op jit(solution)/shard_map/psum | solution.py:25
  99.8 218.5 %all-gather.5.cloned.1.call-start = ((), (), s32[]{:S(2)}) async-start(), calls=%async_computation.1 | async-start | bytes 4456448 | tf_op jit(solution)/shard_map/all_gather | solution.py:27
  338.9 1.9 copy-start.1
  664.6 0.7 copy-start.2
Sparse Core Ops, SparseCore 0:
  11.2 77.4 all-gather.2
  99.9 138.4 all-reduce.3
  240.5 77.7 all-gather.4
where the time goes:
time: 678 us; the launch traced here: 672 us
  waiting for transfers between devices  295 us (44%)
  other arithmetic  268 us (40%)
  matrix products  46.6 us (7%)
  local copies, waits for them, and re-layouts  41.7 us (6%)
  between operations  20.2 us (3%)
    another operation x30, other arithmetic, on_device(): factor = jnp.linalg.cholesky(panel_gram)  172 us
    psum x1, waiting for transfers between devices, on_device(): panel_sum, rest_sum = lax.psum((panel_part, rest_part), 'ex')  139 us
    another operation x3, other arithmetic, on_device(): lax.linalg.triangular_solve(factor, rest_gram, left_side=False, lower=Tru...  85.2 us
    all_gather x1, waiting for transfers between devices, on_device(): panel_rows = lax.all_gather(panel_sum, 'fac', axis=0, tiled=True)  78.9 us
    all_gather x1, waiting for transfers between devices, on_device(): panel_feats = lax.all_gather(own_panel, 'fac', axis=1, tiled=True)  77.6 us
    another operation x14, matrix products, on_device(): factor = jnp.linalg.cholesky(panel_gram)  23 us
    another operation x24, local copies, waits for them, and re-layouts  23 us
  transfers between devices with their start and end apart: 3, of which 3 were waited for; matrix products, arithmetic and copies ran while one was open for 0% of the time, Pallas kernels for 0%

commit v1 on v0

v1 whole, which is shorter than its diff:
```python
import jax
import jax.numpy as jnp
from jax import lax
from jax.experimental import pallas as pl
from jax.experimental.pallas import tpu as pltpu
from jax.sharding import PartitionSpec as P

F32, BF16 = jnp.float32, jnp.bfloat16
N, B, MB, RR = 1024, 128, 16, 32

def split(x):
    hi = x.astype(BF16)
    return hi, (x - hi.astype(F32)).astype(BF16)

def dot_nt(a, b):
    return lax.dot_general(a, b, (((1,), (1,)), ((), ())), preferred_element_type=F32)

def dot_tn(a, b):
    return lax.dot_general(a, b, (((0,), (0,)), ((), ())), preferred_element_type=F32)

def factor(w):
    sub8 = lax.broadcasted_iota(jnp.int32, (8, B), 0)
    for m in range(B // MB):
        r0 = m * MB
        R = [[w[r0 + 8 * i:r0 + 8 * i + 8, B * h:B * h + B] for h in range(2)] for i in range(MB // 8)]
        C = [[jnp.broadcast_to(R[i][0][:, r0 + t:r0 + t + 1], (8, B)) if 8 * i + 7 >= t else None for i in range(MB // 8)] for t in range(MB)]
        S = [None] * (MB // 8)
        for j in range(MB):
            q, p = divmod(j, 8)
            d = jnp.broadcast_to(C[j][q][p:p + 1, :], (8, B))
            inv = 1.0 / d
            s = lax.rsqrt(d)
            S[q] = s if p == 0 else jnp.where(sub8 >= p, s, S[q])
            rows = [jnp.broadcast_to(R[q][h][p:p + 1, :], (8, B)) for h in range(2)]
            for i in range(q, MB // 8):
                mult = C[j][i] * inv
                if i == q:
                    if p == 7:
                        continue
                    mult = jnp.where(sub8 > p, mult, 0.0)
                for h in range(2):
                    R[i][h] = R[i][h] - mult * rows[h]
                for t in range(j + 1, MB):
                    if C[t][i] is not None:
                        qt, pt = divmod(t, 8)
                        C[t][i] = C[t][i] - mult * jnp.broadcast_to(C[j][qt][pt:pt + 1, :], (8, B))
        U = jnp.concatenate([jnp.concatenate([R[i][0] * S[i], R[i][1] * S[i]], axis=1) for i in range(MB // 8)], axis=0)
        w[r0:r0 + MB, :] = U
        if r0 + MB < B:
            hi, lo = split(U)
            lhs = jnp.concatenate([hi[:, :B], hi[:, :B], lo[:, :B]], axis=0)
            rhs = jnp.concatenate([hi, lo, hi], axis=0)
            upd = dot_tn(lhs, rhs)
            w[r0 + MB:, :] = w[r0 + MB:, :] - upd[r0 + MB:, :]

def factor_kernel(g_ref, rest_ref, l_ref, ro_ref, w, pan, hi_s, lo_s):
    ri = lax.broadcasted_iota(jnp.int32, (B, B), 0)
    ci = lax.broadcasted_iota(jnp.int32, (B, B), 1)
    eye = (ri == ci).astype(F32)
    def step(j, _):
        for c in range(N // B):
            @pl.when(j == c)
            def _():
                r0, K = c * B, c * B
                a = g_ref[r0:, r0:r0 + B]
                b = rest_ref[:, r0:r0 + B]
                a = jnp.concatenate([a, b], axis=0)
                if K:
                    rh, rl = hi_s[r0:r0 + B, :K], lo_s[r0:r0 + B, :K]
                    x = dot_nt(hi_s[r0:, :K], jnp.concatenate([rh, rl], axis=0))
                    a = a - (x[:, :B] + x[:, B:] + dot_nt(lo_s[r0:, :K], rh))
                pan[r0:, :] = a
                w[:, :B] = a[:B, :]
                w[:, B:] = eye
        factor(w)
        for c in range(N // B):
            @pl.when(j == c)
            def _():
                r0 = c * B
                th, tl = split(w[:, B:])
                ah, al = split(pan[r0:, :])
                x = dot_nt(ah, jnp.concatenate([th, tl], axis=0))
                lp = x[:, :B] + x[:, B:] + dot_nt(al, th)
                diag = jnp.where(ri >= ci, lp[:B], 0.0)
                lp = jnp.concatenate([diag, lp[B:]], axis=0)
                h, l = split(lp)
                hi_s[r0:, r0:r0 + B] = h
                lo_s[r0:, r0:r0 + B] = l
                l_ref[r0:, r0:r0 + B] = lp[:N - r0]
                ro_ref[:, r0:r0 + B] = lp[N - r0:]
                if c:
                    l_ref[:r0, r0:r0 + B] = jnp.zeros((r0, B), F32)
        return 0
    lax.fori_loop(0, N // B, step, 0)

def factor_and_solve(g, rest):
    return pl.pallas_call(factor_kernel,
        out_shape=(jax.ShapeDtypeStruct((N, N), F32), jax.ShapeDtypeStruct((RR, N), F32)),
        in_specs=[pl.BlockSpec(memory_space=pltpu.VMEM)] * 2,
        out_specs=(pl.BlockSpec(memory_space=pltpu.VMEM),) * 2,
        scratch_shapes=[pltpu.VMEM((B, 2 * B), F32), pltpu.VMEM((N + RR, B), F32),
                        pltpu.VMEM((N + RR, N), BF16), pltpu.VMEM((N + RR, N), BF16)],
        compiler_params=pltpu.CompilerParams(vmem_limit_bytes=48 * 2**20),
    )(g, rest)


def on_device(samples, counts, panel_weight, rest_weight):
    rows = samples.shape[0]
    total = rows * lax.axis_size("ex")
    live = (jnp.arange(rows, dtype=jnp.int32) < counts[0])[:, None]
    own_width = panel_weight.shape[1]

    def features_of(weight):
        return jnp.where(
            live, jax.nn.relu(jnp.dot(samples, weight, preferred_element_type=F32)), 0.0
        ).astype(BF16)

    own_panel = features_of(panel_weight)
    panel_feats = lax.all_gather(own_panel, "fac", axis=1, tiled=True)
    rest_feats = features_of(rest_weight)
    dims = (((0,), (0,)), ((), ()))
    panel_part = lax.dot_general(own_panel, panel_feats, dims, preferred_element_type=F32)
    share = rest_feats.shape[1] // lax.axis_size("ex")
    rest_part = lax.dot_general(rest_feats, panel_feats, dims, preferred_element_type=F32)
    panel_sum, rest_sum = lax.psum((panel_part, rest_part), "ex")
    rest_rows = lax.dynamic_slice_in_dim(rest_sum, lax.axis_index("ex") * share, share, 0)
    panel_rows = lax.all_gather(panel_sum, "fac", axis=0, tiled=True)
    panel_gram = panel_rows / total + jnp.eye(panel_rows.shape[0], dtype=F32)
    rest_gram = jnp.pad(rest_rows / total, ((0, RR - share), (0, 0)))
    factor, rest_factor = factor_and_solve(panel_gram, rest_gram)
    panel_factor = lax.dynamic_slice_in_dim(factor, lax.axis_index("fac") * own_width, own_width, 0)
    return (panel_factor, rest_factor[:share])


def solution(mesh):
    in_specs = (P("ex", None), P("ex"), P(None, "fac"), P(None, "fac"))
    out_specs = (P("fac", None), P(("fac", "ex"), None))
    return jax.shard_map(
        on_device, mesh=mesh, in_specs=in_specs, out_specs=out_specs, check_vma=False
    )
```

time: 678 us -> 368 us (0.54)
  the two profiles are of different devices: /device:TPU:6 before, /device:TPU:4 now
where the time goes in v1:
time: 368 us; the launch traced here: 367 us
  waiting for transfers between devices  295 us (80%)
  Pallas kernels  36.2 us (10%)
  between operations  14.6 us (4%)
  matrix products  13.4 us (4%)
  other arithmetic  5.95 us (2%)
    psum x1, waiting for transfers between devices, on_device(): panel_sum, rest_sum = lax.psum((panel_part, rest_part), 'ex')  137 us
    all_gather x1, waiting for transfers between devices, on_device(): panel_rows = lax.all_gather(panel_sum, 'fac', axis=0, tiled=True)  80.4 us
    all_gather x1, waiting for transfers between devices, on_device(): panel_feats = lax.all_gather(own_panel, 'fac', axis=1, tiled=True)  77.6 us
    pallas_call x1, Pallas kernels, factor_and_solve(): pl.pallas_call(factor_kernel, out_shape=(jax.ShapeDtypeStruct((N, N), F32...  36.2 us
    dot_general x1, matrix products, on_device(): lax.dot_general(rest_feats, panel_feats, dims, preferred_element_type=F32)  7.89 us
  transfers between devices with their start and end apart: 3, of which 3 were waited for; matrix products, arithmetic and copies ran while one was open for 0% of the time, Pallas kernels for 0%

profile of v1, /device:TPU:4, one launch (start us, length us, event | category | flops | bytes accessed | tf_op | source)
XLA Modules:
  0.0 367.5 jit_solution(2983550693134894946)
XLA Ops:
  7.2 0.0 copy-start
  7.2 0.0 all-gather.3.cloned.1.call-start
  8.0 0.8 copy-done
  8.8 0.0 copy-start.1
  8.8 2.4 fusion.1
  11.2 0.0 all-gather.3.cloned.1.call-update
  11.2 0.0 all-reduce.4.cloned.1.call-start
  11.3 77.6 %all-gather.3.cloned.1.call-done = bf16[1024,1024]{0,1:T(8,128)(2,1)} async-done(((bf16[1024,64]{0,1:T(8,128)(2,1)}), bf16[1024,1024]{0,1:T(8,128)(2,1)}) %all-gather.3.cloned.1.call-update) | async-done | bytes 2097168 | tf_op jit(solution)/shard_map/all_gather | solution.py:119
  88.9 3.1 fusion.4
  92.0 0.0 copy-done.1
  92.0 7.9 %fusion.2 = f32[704,1024]{1,0:T(8,128)} fusion(bf16[1024,1024]{0,1:T(8,128)(2,1)} %all-gather.3.cloned.1.call-done, bf16[1024,1024]{1,0:T(8,128)(2,1)S(1)} %copy-done, bf16[1024,704]{0,1:T(8,128)(2,1)S(1)} %copy-done.1, pred[1024]{0:T(1024)(128)(4,1)S(1)} %iota_compare_fusion.1), kind=kOutput, calls=%fused_computation.6 | convolution fusion | flops 2954952704 | bytes 8520704 | tf_op jit(solution)/shard_map/dot_general | solution.py:124
  99.9 0.0 all-reduce.4.cloned.1.call-update
  100.0 0.0 all-gather.5.cloned.1.call-start
  100.0 137.0 %all-reduce.4.cloned.1.call-done = (f32[64,1024]{1,0:T(8,128)}, f32[704,1024]{1,0:T(8,128)}) async-done(((f32[64,1024]{1,0:T(8,128)}, f32[704,1024]{1,0:T(8,128)}), (f32[64,1024]{1,0:T(8,128)}, f32[704,1024]{1,0:T(8,128)})) %all-reduce.4.cloned.1.call-update) | async-done | bytes 3145744 | tf_op jit(solution)/shard_map/psum | solution.py:125
  237.0 0.0 all-gather.5.cloned.1.call-update
  237.0 0.9 dynamic-slice_multiply_fusion
  238.0 80.4 %all-gather.5.cloned.1.call-done = f32[1024,1024]{1,0:T(8,128)} async-done(((f32[64,1024]{1,0:T(8,128)}), f32[1024,1024]{1,0:T(8,128)}) %all-gather.5.cloned.1.call-update) | async-done | bytes 4194320 | tf_op jit(solution)/shard_map/all_gather | solution.py:127
  318.4 5.0 %convert_add_fusion.g_ref = f32[1024,1024]{1,0:T(8,128)} fusion(f32[1024,1024]{1,0:T(8,128)} %all-gather.5.cloned.1.call-done), kind=kLoop, calls=%fused_computation | loop fusion | flops 4194304 | bytes 8388608 | tf_op jit(solution)/shard_map/add | solution.py:128
  323.4 36.2 %shard_map.59 = (f32[1024,1024]{1,0:T(8,128)S(1)}, f32[32,1024]{1,0:T(8,128)S(1)}) custom-call(f32[1024,1024]{1,0:T(8,128)} %convert_add_fusion.g_ref, f32[32,1024]{1,0:T(8,128)S(1)} %pad.4.rest_ref), custom_call_target="tpu_custom_call" | custom-call | tf_op jit(solution)/shard_map/pallas_call | solution.py:97
  359.6 0.7 slice.3
  360.3 0.7 constant_dynamic-slice_fusion
  (2 shorter events, 0.0 us)
Async XLA Ops:
  7.2 1.6 copy-start
  7.2 81.7 %all-gather.3.cloned.1.call-start = ((), (), s32[]{:S(2)}) async-start(), calls=%async_computation | async-start | bytes 2228224 | tf_op jit(solution)/shard_map/all_gather | solution.py:119
  8.8 83.3 %copy-start.1 = (bf16[1024,704]{0,1:T(8,128)(2,1)S(1)}, bf16[1024,704]{0,1:T(8,128)(2,1)}, u32[]{:S(2)}) copy-start(bf16[1024,704]{0,1:T(8,128)(2,1)} %param.7) | copy-start | bytes 4325380
  11.2 225.8 %all-reduce.4.cloned.1.call-start = ((), (), s32[]{:S(2)}) async-start(), calls=%async_computation.2 | async-start | bytes 6291456 | tf_op jit(solution)/shard_map/psum | solution.py:125
  100.0 218.4 %all-gather.5.cloned.1.call-start = ((), (), s32[]{:S(2)}) async-start(), calls=%async_computation.1 | async-start | bytes 4456448 | tf_op jit(solution)/shard_map/all_gather | solution.py:127
Sparse Core Ops, SparseCore 0:
  11.3 77.5 all-gather.2
  100.1 136.8 all-reduce.3
  239.1 79.2 all-gather.4

commit v2 on v1

--- a/solution.py
+++ b/solution.py
@@ -1,3 +1,5 @@
+import functools
+
 import jax
 import jax.numpy as jnp
 from jax import lax
@@ -7,6 +9,8 @@
 
 F32, BF16 = jnp.float32, jnp.bfloat16
 N, B, MB, RR = 1024, 128, 16, 32
+DIN, NE, NZ, NQ = 1024, 32, 16, 16
+MESH = pl.DeviceIdType.MESH
 
 def split(x):
     hi = x.astype(BF16)
@@ -14,6 +18,9 @@
 
 def dot_nt(a, b):
     return lax.dot_general(a, b, (((1,), (1,)), ((), ())), preferred_element_type=F32)
+
+def dot_nn(a, b):
+    return jnp.dot(a, b, preferred_element_type=F32)
 
 def dot_tn(a, b):
     return lax.dot_general(a, b, (((0,), (0,)), ((), ())), preferred_element_type=F32)
@@ -53,7 +60,7 @@
             upd = dot_tn(lhs, rhs)
             w[r0 + MB:, :] = w[r0 + MB:, :] - upd[r0 + MB:, :]
 
-def factor_kernel(g_ref, rest_ref, l_ref, ro_ref, w, pan, hi_s, lo_s):
+def factor_kernel(scale, g_ref, rest_ref, l_ref, ro_ref, w, pan, hi_s, lo_s):
     ri = lax.broadcasted_iota(jnp.int32, (B, B), 0)
     ci = lax.broadcasted_iota(jnp.int32, (B, B), 1)
     eye = (ri == ci).astype(F32)
@@ -62,9 +69,8 @@
             @pl.when(j == c)
             def _():
                 r0, K = c * B, c * B
-                a = g_ref[r0:, r0:r0 + B]
-                b = rest_ref[:, r0:r0 + B]
-                a = jnp.concatenate([a, b], axis=0)
+                a = g_ref[c, r0:, :] * scale
+                a = jnp.concatenate([a[:B] + eye] + ([a[B:]] if r0 + B < N else []) + [rest_ref[:, r0:r0 + B] * scale], axis=0)
                 if K:
                     rh, rl = hi_s[r0:r0 + B, :K], lo_s[r0:r0 + B, :K]
                     x = dot_nt(hi_s[r0:, :K], jnp.concatenate([rh, rl], axis=0))
@@ -93,8 +99,8 @@
         return 0
     lax.fori_loop(0, N // B, step, 0)
 
-def factor_and_solve(g, rest):
-    return pl.pallas_call(factor_kernel,
+def factor_and_solve(g, rest, scale):
+    return pl.pallas_call(functools.partial(factor_kernel, scale),
         out_shape=(jax.ShapeDtypeStruct((N, N), F32), jax.ShapeDtypeStruct((RR, N), F32)),
         in_specs=[pl.BlockSpec(memory_space=pltpu.VMEM)] * 2,
         out_specs=(pl.BlockSpec(memory_space=pltpu.VMEM),) * 2,
@@ -104,30 +110,223 @@
     )(g, rest)
 
 
+SEL = 24
+
+
+def gram_kernel(shares, x_ref, n_ref, wp_ref, wr_ref, gb, rest_out, xs, wo, wt, pf, wrt, rft, pt, part, prec, zb, rsend, rrecv, sems):
+    e, z = lax.axis_index("ex"), lax.axis_index("fac")
+    chip, core = e // 2, e % 2
+    mate = chip * 2 + 1 - core
+    rows = x_ref.shape[0]
+    (s_w, r_w, s_p, r_p, s_m, r_m, s_g, r_g, s_z, r_z, s_a, r_a, s_b, r_b, s_r, r_r) = sems
+
+    def z_peer(k):
+        return {"fac": (z + k) % NZ}
+
+    def e_peer(k):
+        return {"ex": (e + k) % NE}
+
+    def chip_peer(k):
+        return {"ex": ((chip + k) % NQ) * 2 + core}
+
+    def each(lo, hi, body):
+        def run(k, _):
+            body(k)
+            return 0
+        lax.fori_loop(lo, hi, run, 0)
+
+    barrier = pltpu.get_barrier_semaphore()
+    each(1, NZ, lambda k: pl.semaphore_signal(barrier, inc=1, device_id=z_peer(k), device_id_type=MESH))
+    each(1, NE, lambda k: pl.semaphore_signal(barrier, inc=1, device_id=e_peer(k), device_id_type=MESH))
+
+    own = wp_ref.shape[1]
+    eye = (lax.broadcasted_iota(jnp.int32, (own, own), 0) == lax.broadcasted_iota(jnp.int32, (own, own), 1)).astype(BF16)
+    wt_own = dot_nt(eye, wp_ref[...]).astype(BF16)
+    wo[...] = wt_own.reshape(4, 16, DIN)
+    lanes = pl.ds(pl.multiple_of((e % 8) * 128, 128), 128)
+    wt[z, e // 8, :, lanes] = wo[e // 8, :, lanes]
+    live = lax.broadcasted_iota(jnp.int32, (rows, 1), 0) < n_ref[0]
+    xs[...] = jnp.where(live, x_ref[...].astype(F32), 0.0).astype(BF16)
+
+    def copy(src, dst, send, recv, device):
+        return pltpu.make_async_remote_copy(src, dst, send, recv, device_id=device, device_id_type=MESH)
+
+    pl.semaphore_wait(barrier, NZ - 1 + NE - 1)
+
+    def tile(i):
+        return wt.at[:, i // 8, :, pl.ds(pl.multiple_of((i % 8) * 128, 128), 128)]
+
+    def z_weight(k, src_z):
+        piece = wt.at[src_z, e // 8, :, pl.ds(pl.multiple_of((e % 8) * 128, 128), 128)]
+        return copy(piece, piece, s_w.at[k], r_w.at[k], z_peer(k))
+
+    each(1, NZ, lambda k: z_weight(k, z).start())
+    span = 256
+    wide = wr_ref.shape[1]
+
+    def select(i, _):
+        r0 = pl.multiple_of(i * span, span)
+        c = lax.broadcasted_iota(jnp.int32, (span, 1), 0).astype(F32) + (i * span).astype(F32)
+        b = jnp.floor((c + 0.5) * (1.0 / SEL))
+        want = jnp.where(c - SEL * b < shares, c - (SEL - shares) * b, -1.0)
+        sel = (lax.broadcasted_iota(jnp.int32, (span, wide), 1).astype(F32) == want).astype(BF16)
+        wrt[pl.ds(r0, span), :] = dot_nt(sel, wr_ref[...]).astype(BF16)
+        return 0
+
+    lax.fori_loop(0, NE * SEL // span, select, 0)
+    each(1, NZ, lambda k: z_weight(k, (z + NZ - k) % NZ).wait_recv())
+
+    def plane_weight(k):
+        return copy(tile(e), tile(e), s_p.at[k], r_p.at[k], chip_peer(k))
+
+    def mate_weight(k):
+        i = ((chip + NQ - k) % NQ) * 2 + core
+        return copy(tile(i), tile(i), s_m.at[k], r_m.at[k], {"ex": mate})
+
+    each(1, NQ, lambda k: plane_weight(k).start())
+    mate_weight(0).start()
+
+    def rest_features(i, _):
+        r0 = pl.multiple_of(i * span, span)
+        f = dot_nt(wrt[pl.ds(r0, span), :], xs[...])
+        rft[pl.ds(r0, span), :] = jnp.maximum(f, 0.0).astype(BF16)
+        return 0
+
+    lax.fori_loop(0, NE * SEL // span, rest_features, 0)
+    pt[...] = jnp.maximum(dot_nt(wt_own, xs[...]), 0.0).astype(BF16)
+
+    def pass_on(k):
+        plane_weight(k).wait_recv()
+        mate_weight(k).start()
+
+    each(1, NQ, pass_on)
+    each(0, NQ, lambda k: mate_weight(k).wait_recv())
+
+    def panel_features(i, _):
+        r0 = pl.multiple_of(i * span, span)
+        f = dot_nt(xs[pl.ds(r0, span), :], wt[...].reshape(N, DIN))
+        pf[pl.ds(r0, span), :] = jnp.maximum(f, 0.0).astype(BF16)
+        return 0
+
+    lax.fori_loop(0, rows // span, panel_features, 0)
+
+    mine = dot_nn(pt[...], pf[...])
+    for q in range(4):
+        for h, lt in ((0, q), (1, 7 - q)):
+            part[q * 8:q * 8 + 8, h] = mine[:, lt * 128:lt * 128 + 128].reshape(8, 8, 128)
+
+    def gram_part(k):
+        return copy(part.at[(e + k) % NE], prec.at[k], s_g.at[k], r_g.at[k], e_peer(k))
+
+    each(1, NE, lambda k: gram_part(k).start())
+
+    def rest_gram(i, _):
+        r0 = pl.multiple_of(i * span, span)
+        rsend[pl.ds(r0, span), :] = dot_nn(rft[pl.ds(r0, span), :], pf[...])
+        return 0
+
+    lax.fori_loop(0, NE * SEL // span, rest_gram, 0)
+    each(1, NE, lambda k: gram_part(k).wait_recv())
+    total = lax.fori_loop(1, NE, lambda k, t: t + prec[k], part[e])
+    zb[:, z] = total
+
+    def z_gram(k, src_z):
+        return copy(zb.at[:, src_z], zb.at[:, src_z], s_z.at[k], r_z.at[k], z_peer(k))
+
+    each(1, NZ, lambda k: z_gram(k, z).start())
+    each(1, NZ, lambda k: z_gram(k, (z + NZ - k) % NZ).wait_recv())
+    q, rg = e // 8, e % 8
+    gb[q, :, rg] = zb[0]
+    gb[7 - q, 8:, rg] = zb[1, 8:]
+
+    def left(i):
+        return gb.at[i // 8, :, i % 8]
+
+    def right(i):
+        return gb.at[7 - i // 8, pl.ds(8, 8), i % 8]
+
+    halves = (left, right)
+
+    def plane_gram(h, k):
+        piece = halves[h](e)
+        return copy(piece, piece, s_a.at[h * NQ + k], r_a.at[h * NQ + k], chip_peer(k))
+
+    def mate_gram(h, k):
+        piece = halves[h](((chip + NQ - k) % NQ) * 2 + core)
+        return copy(piece, piece, s_b.at[h * NQ + k], r_b.at[h * NQ + k], {"ex": mate})
+
+    for h in range(2):
+        each(1, NQ, lambda k: plane_gram(h, k).start())
+        mate_gram(h, 0).start()
+
+    def rest_part(k):
+        src = rsend.at[pl.ds(pl.multiple_of(((e + k) % NE) * SEL, 8), SEL), :]
+        return copy(src, rrecv.at[k], s_r.at[k], r_r.at[k], e_peer(k))
+
+    each(1, NE, lambda k: rest_part(k).start())
+
+    for h in range(2):
+        def pass_gram(k):
+            plane_gram(h, k).wait_recv()
+            mate_gram(h, k).start()
+
+        each(1, NQ, pass_gram)
+    for h in range(2):
+        each(0, NQ, lambda k: mate_gram(h, k).wait_recv())
+    each(1, NE, lambda k: rest_part(k).wait_recv())
+    first = rsend[pl.ds(pl.multiple_of(e * SEL, 8), SEL), :]
+    rest_out[:SEL, :] = lax.fori_loop(1, NE, lambda k, t: t + rrecv[k], first)
+    rest_out[SEL:, :] = jnp.zeros((RR - SEL, N), F32)
+
+    each(1, NZ, lambda k: z_weight(k, z).wait_send())
+    each(1, NQ, lambda k: plane_weight(k).wait_send())
+    each(0, NQ, lambda k: mate_weight(k).wait_send())
+    each(1, NE, lambda k: gram_part(k).wait_send())
+    each(1, NZ, lambda k: z_gram(k, z).wait_send())
+
+    for h in range(2):
+        each(1, NQ, lambda k: plane_gram(h, k).wait_send())
+        each(0, NQ, lambda k: mate_gram(h, k).wait_send())
+    each(1, NE, lambda k: rest_part(k).wait_send())
+
+
+def gram(samples, counts, panel_weight, rest_weight):
+    rows = samples.shape[0]
+    own, wide = panel_weight.shape[1], rest_weight.shape[1]
+    vmem = pl.BlockSpec(memory_space=pltpu.VMEM)
+    counted = [NZ, NZ, NQ, NQ, NQ, NQ, NE, NE, NZ, NZ, 2 * NQ, 2 * NQ, 2 * NQ, 2 * NQ, NE, NE]
+    return pl.pallas_call(
+        functools.partial(gram_kernel, wide // NE),
+        out_shape=(jax.ShapeDtypeStruct((8, NZ, 8, 8, 128), F32), jax.ShapeDtypeStruct((RR, N), F32)),
+        in_specs=[vmem, pl.BlockSpec(memory_space=pltpu.SMEM), vmem, vmem],
+        out_specs=(vmem, vmem),
+        scratch_shapes=[
+            pltpu.VMEM((rows, DIN), BF16),
+            pltpu.VMEM((4, 16, DIN), BF16),
+            pltpu.VMEM((NZ, 4, 16, DIN), BF16),
+            pltpu.VMEM((rows, N), BF16),
+            pltpu.VMEM((NE * SEL, DIN), BF16),
+            pltpu.VMEM((NE * SEL, rows), BF16),
+            pltpu.VMEM((own, rows), BF16),
+            pltpu.VMEM((NE, 2, 8, 128), F32),
+            pltpu.VMEM((NE, 2, 8, 128), F32),
+            pltpu.VMEM((2, NZ, 8, 128), F32),
+            pltpu.VMEM((NE * SEL, N), F32),
+            pltpu.VMEM((NE, SEL, N), F32),
+            [pltpu.SemaphoreType.DMA((c,)) for c in counted],
+        ],
+        compiler_params=pltpu.CompilerParams(
+            collective_id=0, has_side_effects=True, vmem_limit_bytes=48 * 2**20
+        ),
+        cost_estimate=pl.CostEstimate(flops=8 * 2**30, bytes_accessed=8 * 2**20, transcendentals=0),
+    )(samples, counts, panel_weight, rest_weight)
+
+
 def on_device(samples, counts, panel_weight, rest_weight):
-    rows = samples.shape[0]
-    total = rows * lax.axis_size("ex")
-    live = (jnp.arange(rows, dtype=jnp.int32) < counts[0])[:, None]
-    own_width = panel_weight.shape[1]
-
-    def features_of(weight):
-        return jnp.where(
-            live, jax.nn.relu(jnp.dot(samples, weight, preferred_element_type=F32)), 0.0
-        ).astype(BF16)
-
-    own_panel = features_of(panel_weight)
-    panel_feats = lax.all_gather(own_panel, "fac", axis=1, tiled=True)
-    rest_feats = features_of(rest_weight)
-    dims = (((0,), (0,)), ((), ()))
-    panel_part = lax.dot_general(own_panel, panel_feats, dims, preferred_element_type=F32)
-    share = rest_feats.shape[1] // lax.axis_size("ex")
-    rest_part = lax.dot_general(rest_feats, panel_feats, dims, preferred_element_type=F32)
-    panel_sum, rest_sum = lax.psum((panel_part, rest_part), "ex")
-    rest_rows = lax.dynamic_slice_in_dim(rest_sum, lax.axis_index("ex") * share, share, 0)
-    panel_rows = lax.all_gather(panel_sum, "fac", axis=0, tiled=True)
-    panel_gram = panel_rows / total + jnp.eye(panel_rows.shape[0], dtype=F32)
-    rest_gram = jnp.pad(rest_rows / total, ((0, RR - share), (0, 0)))
-    factor, rest_factor = factor_and_solve(panel_gram, rest_gram)
+    total = samples.shape[0] * NE
+    share, own_width = rest_weight.shape[1] // NE, panel_weight.shape[1]
+    panel_gram, rest_gram = gram(samples, counts, panel_weight, rest_weight)
+    factor, rest_factor = factor_and_solve(panel_gram.reshape(8, N, 128), rest_gram, 1.0 / total)
     panel_factor = lax.dynamic_slice_in_dim(factor, lax.axis_index("fac") * own_width, own_width, 0)
     return (panel_factor, rest_factor[:share])
 

time: 368 us -> 179 us (0.49)
  the two profiles are of different devices: /device:TPU:4 before, /device:TPU:1 now
where the time goes in v2:
time: 179 us; the launch traced here: 178 us
  Pallas kernels  168 us (94%)
  local copies, waits for them, and re-layouts  8.6 us (5%)
    pallas_call x1, Pallas kernels, gram(): pl.pallas_call(functools.partial(gram_kernel, wide // NE), out_shape=(jax...  132 us
    pallas_call x1, Pallas kernels, factor_and_solve(): pl.pallas_call(functools.partial(factor_kernel, scale), out_shape=(jax.Sh...  36.2 us
    unnamed x6, local copies, waits for them, and re-layouts  6.29 us

profile of v2, /device:TPU:1, one launch (start us, length us, event | category | flops | bytes accessed | tf_op | source)
XLA Modules:
  0.0 178.4 jit_solution(4127538993451602543)
XLA Ops:
  1.3 1.1 copy.6.wp_ref
  2.4 1.7 copy.7.wr_ref
  4.1 0.0 copy-start.1
  4.1 1.6 copy-done.1
  5.6 132.3 %shard_map.59 = (f32[8,16,8,8,128]{4,3,2,1,0:T(8,128)}, f32[32,1024]{1,0:T(8,128)S(1)}) custom-call(bf16[1024,1024]{1,0:T(8,128)(2,1)S(1)} %copy-done.1, s32[1]{0:T(128)S(6)} %copy.8.n_ref, bf16[1024,64]{1,0:T(8,128)(2,1)S(1)} %copy.6.wp_ref, bf16[1024,704]{1,0:T(8,128)(2,1)S(1)} %copy.7.wr_ref), custom_call_target="tpu_custom_call" | custom-call | flops 8589934592 | bytes 8388608 | tf_op jit(solution)/shard_map/pallas_call | solution.py:298
  138.0 36.2 %shard_map.60 = (f32[1024,1024]{1,0:T(8,128)S(1)}, f32[32,1024]{1,0:T(8,128)S(1)}) custom-call(f32[8,1024,128]{2,1,0:T(8,128)} %bitcast.1, f32[32,1024]{1,0:T(8,128)S(1)} %get-tuple-element.7.rest_ref), custom_call_target="tpu_custom_call" | custom-call | tf_op jit(solution)/shard_map/pallas_call | solution.py:103
  174.1 0.0 copy-start
  174.1 1.9 %copy-done = f32[1024,1024]{1,0:T(8,128)} copy-done((f32[1024,1024]{1,0:T(8,128)}, f32[1024,1024]{1,0:T(8,128)S(1)}, u32[]{:S(2)}) %copy-start) | copy-done | bytes 4194328
  176.1 1.7 constant_dynamic-slice_fusion
  177.8 0.6 slice.3
Async XLA Ops:
  4.1 1.6 copy-start.1
  174.1 1.9 %copy-start = (f32[1024,1024]{1,0:T(8,128)}, f32[1024,1024]{1,0:T(8,128)S(1)}, u32[]{:S(2)}) copy-start(f32[1024,1024]{1,0:T(8,128)S(1)} %get-tuple-element.8) | copy-start | bytes 12582916

commit v3 on v0

v3 whole, which is shorter than its diff:
```python
import functools

import jax
import jax.numpy as jnp
from jax import lax
from jax.experimental import pallas as pl
from jax.experimental.pallas import tpu as pltpu
from jax.sharding import PartitionSpec as P

F32, BF16 = jnp.float32, jnp.bfloat16
MESH = pl.DeviceIdType.MESH
N, DIN, B, MB = 1024, 1024, 128, 16
NE, NZ, NQ = 32, 16, 16
SEL = 24
HALF = NQ * SEL


def split(x):
    hi = x.astype(BF16)
    return hi, (x - hi.astype(F32)).astype(BF16)


def dot_nt(a, b):
    return lax.dot_general(a, b, (((1,), (1,)), ((), ())), preferred_element_type=F32)


def dot_nn(a, b):
    return jnp.dot(a, b, preferred_element_type=F32)


def dot_tn(a, b):
    return lax.dot_general(a, b, (((0,), (0,)), ((), ())), preferred_element_type=F32)


def factor(w):
    row = lax.broadcasted_iota(jnp.int32, (MB, B), 0)
    for m in range(B // MB):
        r0 = m * MB
        R = w[r0:r0 + MB, :]
        C = jnp.stack([jnp.broadcast_to(R[:, r0 + t:r0 + t + 1], (MB, B)) for t in range(MB)], axis=0)
        S = jnp.ones((MB, B), F32)
        for j in range(MB):
            c = C[0]
            d = jnp.broadcast_to(c[j:j + 1, :], (MB, B))
            S = jnp.where(row >= j, lax.rsqrt(d), S)
            if j < MB - 1:
                mult = jnp.where(row > j, c * (1.0 / d), 0.0)
                R = R - jnp.concatenate([mult, mult], axis=1) * R[j:j + 1, :]
                C = C[1:] - mult[None] * C[1:, j:j + 1, :]
        U = R * jnp.concatenate([S, S], axis=1)
        w[r0:r0 + MB, :] = U
        if r0 + MB < B:
            hi, lo = split(U)
            lhs = jnp.concatenate([hi[:, :B], hi[:, :B], lo[:, :B]], axis=0)
            rhs = jnp.concatenate([hi, lo, hi], axis=0)
            upd = dot_tn(lhs, rhs)
            w[r0 + MB:, :] = w[r0 + MB:, :] - upd[r0 + MB:, :]


def times_split(hi, lo, b2):
    x = dot_nt(hi, b2)
    return x[:, :B] + x[:, B:] + dot_nt(lo, b2[:B])


def kernel(share, scale, x_ref, n_ref, wp_ref, wr_ref, panel_out, rest_out,
           xs, wr, wt, pf, wrt, rft, pt, part, prec, zb, gb, rsend, rmate, rrecv, w, pan, hi_s, lo_s, tts, xh, xl, loc, sems):
    e, z = lax.axis_index("ex"), lax.axis_index("fac")
    chip, core = e // 2, e % 2
    mate = {"ex": chip * 2 + 1 - core}
    lq, rg, zg = e // 8, e % 8, z // 4
    rows, own, wide = xs.shape[0], wp_ref.shape[0], wr_ref.shape[0]
    (s_w, r_w, s_p, r_p, s_m, r_m, s_g, r_g, s_z, r_z, s_a, r_a, s_b, r_b, s_r, r_r, s_h, r_h) = sems

    def z_peer(k):
        return {"fac": (z + k) % NZ}

    def e_peer(k):
        return {"ex": (e + k) % NE}

    def chip_peer(k):
        return {"ex": ((chip + k) % NQ) * 2 + core}

    def chip_from(k):
        return ((chip + NQ - k) % NQ) * 2 + core

    def each(lo, hi, body):
        def run(k, _):
            body(k)
            return 0
        lax.fori_loop(lo, hi, run, 0)

    def blocks(count, span, body):
        each(0, count, lambda i: body(pl.ds(pl.multiple_of(i * span, span), span)))

    def copy(src, dst, send, recv, device):
        return pltpu.make_async_remote_copy(src, dst, send, recv, device_id=device, device_id_type=MESH)

    def lanes(i):
        return pl.ds(pl.multiple_of((i % 8) * 128, 128), 128)

    barrier = pltpu.get_barrier_semaphore()
    each(1, NZ, lambda k: pl.semaphore_signal(barrier, inc=1, device_id=z_peer(k), device_id_type=MESH))
    each(1, NE, lambda k: pl.semaphore_signal(barrier, inc=1, device_id=e_peer(k), device_id_type=MESH))
    own_tile = wp_ref.at[pl.ds(pl.multiple_of((e // 8) * 16, 16), 16), lanes(e)]
    local = [
        pltpu.make_async_copy(own_tile, wt.at[z, e // 8, :, lanes(e)], loc.at[0]),
        pltpu.make_async_copy(x_ref, xs, loc.at[1]),
        pltpu.make_async_copy(wr_ref, wr, loc.at[2]),
        pltpu.make_async_copy(wp_ref, pt, loc.at[3]),
    ]
    for c in local:
        c.start()
    pl.semaphore_wait(barrier, NZ - 1 + NE - 1)

    def tile(i):
        return wt.at[:, i // 8, :, lanes(i)]

    def z_weight(k, src_z):
        return copy(own_tile, wt.at[src_z, e // 8, :, lanes(e)], s_w.at[k], r_w.at[k], z_peer(k))

    each(1, NZ, lambda k: z_weight(k, z).start())
    for c in local:
        c.wait()

    def mask(at):
        live = lax.broadcasted_iota(jnp.int32, (256, 1), 0) + at.start < n_ref[0]
        xs[at, :] = jnp.where(live, xs[at, :].astype(F32), 0.0).astype(BF16)

    blocks(rows // 256, 256, mask)

    def select(at):
        c = (lax.broadcasted_iota(jnp.int32, (128, 1), 0) + at.start).astype(F32)
        b = jnp.floor((c + 0.5) * (1.0 / SEL))
        t = c - SEL * b
        device = jnp.where(b < NQ, 2 * b, 2 * (b - NQ) + 1)
        want = jnp.where(t < share, device * share + t, -1.0)
        sel = (lax.broadcasted_iota(jnp.int32, (128, wide), 1).astype(F32) == want).astype(BF16)
        wrt[at, :] = dot_nn(sel, wr[...]).astype(BF16)

    blocks(NE * SEL // 128, 128, select)
    each(1, NZ, lambda k: z_weight(k, (z + NZ - k) % NZ).wait_recv())

    def plane_weight(k):
        return copy(tile(e), tile(e), s_p.at[k], r_p.at[k], chip_peer(k))

    def mate_weight(k):
        i = chip_from(k)
        return copy(tile(i), tile(i), s_m.at[k], r_m.at[k], mate)

    each(1, NQ, lambda k: plane_weight(k).start())
    mate_weight(0).start()

    def rest_features(at):
        rft[at, :] = jnp.maximum(dot_nt(wrt[at, :], xs[...]), 0.0).astype(BF16)

    blocks(NE * SEL // 256, 256, rest_features)
    pt[...] = jnp.maximum(dot_nt(pt[...], xs[...]), 0.0).astype(BF16)

    def pass_on(k):
        plane_weight(k).wait_recv()
        mate_weight(k).start()

    each(1, NQ, pass_on)
    each(0, NQ, lambda k: mate_weight(k).wait_recv())

    def panel_features(at):
        pf[at, :] = jnp.maximum(dot_nt(xs[at, :], wt[...].reshape(N, DIN)), 0.0).astype(BF16)

    blocks(rows // 256, 256, panel_features)

    mine = dot_nn(pt[...], pf[...])
    for lt in range(8):
        part[lt // 4, lt % 4] = mine[:, lt * 128:lt * 128 + 128].reshape(8, 8, 128)

    def gram_part(k):
        i = (e + k) % NE
        return copy(part.at[:, (i // 8 + 4 - zg) % 4, i % 8], prec.at[k], s_g.at[k], r_g.at[k], e_peer(k))

    each(1, NE, lambda k: gram_part(k).start())

    def rest_gram(c):
        at = pl.ds(pl.multiple_of(c * HALF, HALF), HALF)
        rsend[c] = dot_nn(rft[at, :], pf[...]).reshape(NQ, SEL, N)

    rest_half = copy(rsend.at[1 - core], rmate, s_h.at[0], r_h.at[0], mate)
    rest_gram(1 - core)
    rest_half.start()
    each(1, NE, lambda k: gram_part(k).wait_recv())
    zb[:, z] = lax.fori_loop(1, NE, lambda k, t: t + prec[k], part[:, (lq + 4 - zg) % 4, rg])

    def z_gram(k, src_z):
        return copy(zb.at[:, src_z], zb.at[:, src_z], s_z.at[k], r_z.at[k], z_peer(k))

    each(1, NZ, lambda k: z_gram(k, z).start())
    rest_gram(core)
    each(1, NZ, lambda k: z_gram(k, (z + NZ - k) % NZ).wait_recv())

    def group(i, lt):
        return (i // 8 + 8 - lt) % 4

    def needed(i, lt, run):
        pl.when(group(i, lt) >= lt // 2)(run)

    def panel_piece(i, lt):
        return gb.at[lt, pl.ds(group(i, lt) * 4, 4), i % 8]

    def plane_gram(lt, k):
        src = zb.at[lt // 4, pl.ds(group(e, lt) * 4, 4)]
        return copy(src, panel_piece(e, lt), s_a.at[lt * NQ + k], r_a.at[lt * NQ + k], chip_peer(k))

    def from_plane(lt, k):
        piece = panel_piece(chip_from(k), lt)
        return copy(piece, piece, s_a.at[lt * NQ + k], r_a.at[lt * NQ + k], chip_peer(k))

    def mate_gram(lt, k):
        piece = panel_piece(chip_from(k), lt)
        return copy(piece, piece, s_b.at[lt * NQ + k], r_b.at[lt * NQ + k], mate)

    def from_mate(lt, k):
        piece = panel_piece(((chip + NQ - k) % NQ) * 2 + 1 - core, lt)
        return copy(piece, piece, s_b.at[lt * NQ + k], r_b.at[lt * NQ + k], mate)

    def send_panel(lt):
        def run():
            gb[lt, pl.ds(group(e, lt) * 4, 4), rg] = zb[lt // 4, pl.ds(group(e, lt) * 4, 4)]
            each(1, NQ, lambda k: plane_gram(lt, k).start())
            mate_gram(lt, 0).start()
        needed(e, lt, run)

    each(0, N // B, send_panel)

    rest_half.wait_recv()

    def add_mate(i):
        rsend[core, i] = rsend[core, i] + rmate[i]

    each(0, NQ, add_mate)

    def rest_part(k):
        return copy(rsend.at[core, (chip + k) % NQ], rrecv.at[k], s_r.at[k], r_r.at[k], chip_peer(k))

    each(1, NQ, lambda k: rest_part(k).start())

    def pass_panel(lt):
        def run(k):
            def go():
                from_plane(lt, k).wait_recv()
                mate_gram(lt, k).start()
            needed(chip_from(k), lt, go)
        each(1, NQ, run)

    def wait_panel(lt):
        def run(k):
            needed(((chip + NQ - k) % NQ) * 2 + 1 - core, lt, lambda: from_mate(lt, k).wait_recv())
        each(0, NQ, run)

    ri = lax.broadcasted_iota(jnp.int32, (B, B), 0)
    ci = lax.broadcasted_iota(jnp.int32, (B, B), 1)
    eye = (ri == ci).astype(F32)
    pass_panel(0)

    def step(j):
        wait_panel(j)
        for c in range(N // B):
            @pl.when(j == c)
            def _():
                r0 = c * B
                a = gb[c, 2 * c:].reshape(N - r0, B) * scale
                a = jnp.concatenate([a[:B] + eye] + ([a[B:]] if r0 + B < N else []), axis=0)
                if c:
                    b2 = jnp.concatenate([hi_s[r0:r0 + B, :r0], lo_s[r0:r0 + B, :r0]], axis=0)
                    a = a - times_split(hi_s[r0:, :r0], lo_s[r0:, :r0], b2)
                pan[r0:, :] = a
                w[:, :B] = a[:B, :]
                w[:, B:] = eye

        pl.when(j < N // B - 1)(lambda: pass_panel(j + 1))
        factor(w)
        for c in range(N // B):
            @pl.when(j == c)
            def _():
                r0 = c * B
                t2 = jnp.concatenate(split(w[:, B:]), axis=0)
                tts[c] = t2
                ah, al = split(pan[r0:, :])
                lp = times_split(ah, al, t2)
                lp = jnp.concatenate([jnp.where(ri >= ci, lp[:B], 0.0)] + ([lp[B:]] if r0 + B < N else []), axis=0)
                h, l = split(lp)
                hi_s[r0:, r0:r0 + B] = h
                lo_s[r0:, r0:r0 + B] = l
                pan[r0:, :] = lp
                ours = pan[pl.ds(pl.multiple_of(z * own, own), own), :]
                panel_out[:, r0:r0 + B] = jnp.where(z >= 2 * c, ours, 0.0)

    each(0, N // B, step)

    each(1, NQ, lambda k: rest_part(k).wait_recv())
    total = lax.fori_loop(1, NQ, lambda k, t: t + rrecv[k], rsend[core, chip]) * scale
    for c in range(N // B):
        r0 = c * B
        a = total[:, r0:r0 + B]
        if c:
            b2 = jnp.concatenate([hi_s[r0:r0 + B, :r0], lo_s[r0:r0 + B, :r0]], axis=0)
            a = a - times_split(xh[:SEL, :r0], xl[:SEL, :r0], b2)
        ah, al = split(a)
        a = times_split(ah, al, tts[c])
        rest_out[:, r0:r0 + B] = a[:share]
        h, l = split(a)
        xh[:SEL, r0:r0 + B] = h
        xl[:SEL, r0:r0 + B] = l

    each(1, NZ, lambda k: z_weight(k, z).wait_send())
    each(1, NQ, lambda k: plane_weight(k).wait_send())
    each(0, NQ, lambda k: mate_weight(k).wait_send())
    each(1, NE, lambda k: gram_part(k).wait_send())
    each(1, NZ, lambda k: z_gram(k, z).wait_send())
    rest_half.wait_send()
    each(1, NQ, lambda k: rest_part(k).wait_send())

    def panel_sent(lt):
        needed(e, lt, lambda: each(1, NQ, lambda k: plane_gram(lt, k).wait_send()))
        each(0, NQ, lambda k: needed(chip_from(k), lt, lambda: mate_gram(lt, k).wait_send()))

    each(0, N // B, panel_sent)


def on_device(samples, counts, panel_weight, rest_weight):
    rows = samples.shape[0]
    own, wide = panel_weight.shape[1], rest_weight.shape[1]
    share = wide // NE
    vmem, anywhere = pl.BlockSpec(memory_space=pltpu.VMEM), pl.BlockSpec(memory_space=pl.ANY)
    counted = [NZ, NZ, NQ, NQ, NQ, NQ, NE, NE, NZ, NZ, 8 * NQ, 8 * NQ, 8 * NQ, 8 * NQ, NQ, NQ, 1, 1]
    return pl.pallas_call(
        functools.partial(kernel, share, 1.0 / (rows * NE)),
        out_shape=(jax.ShapeDtypeStruct((own, N), F32), jax.ShapeDtypeStruct((share, N), F32)),
        in_specs=[anywhere, pl.BlockSpec(memory_space=pltpu.SMEM), anywhere, anywhere],
        out_specs=(vmem, vmem),
        scratch_shapes=[
            pltpu.VMEM((rows, DIN), BF16),
            pltpu.VMEM((wide, DIN), BF16),
            pltpu.VMEM((NZ, 4, 16, DIN), BF16),
            pltpu.VMEM((rows, N), BF16),
            pltpu.VMEM((NE * SEL, DIN), BF16),
            pltpu.VMEM((NE * SEL, rows), BF16),
            pltpu.VMEM((own, rows), BF16),
            pltpu.VMEM((2, 4, 8, 8, 128), F32),
            pltpu.VMEM((NE, 2, 8, 128), F32),
            pltpu.VMEM((2, NZ, 8, 128), F32),
            pltpu.VMEM((8, NZ, 8, 8, 128), F32),
            pltpu.VMEM((2, NQ, SEL, N), F32),
            pltpu.VMEM((NQ, SEL, N), F32),
            pltpu.VMEM((NQ, SEL, N), F32),
            pltpu.VMEM((B, 2 * B), F32),
            pltpu.VMEM((N, B), F32),
            pltpu.VMEM((N, N), BF16),
            pltpu.VMEM((N, N), BF16),
            pltpu.VMEM((8, 2 * B, B), BF16),
            pltpu.VMEM((32, N), BF16),
            pltpu.VMEM((32, N), BF16),
            pltpu.SemaphoreType.DMA((4,)),
            [pltpu.SemaphoreType.DMA((c,)) for c in counted],
        ],
        compiler_params=pltpu.CompilerParams(
            collective_id=0, has_side_effects=True, vmem_limit_bytes=52 * 2**20
        ),
        cost_estimate=pl.CostEstimate(flops=10 * 2**30, bytes_accessed=8 * 2**20, transcendentals=0),
    )(samples, counts, panel_weight.T, rest_weight.T)


def solution(mesh):
    in_specs = (P("ex", None), P("ex"), P(None, "fac"), P(None, "fac"))
    out_specs = (P("fac", None), P(("fac", "ex"), None))
    return jax.shard_map(
        on_device, mesh=mesh, in_specs=in_specs, out_specs=out_specs, check_vma=False
    )
```

time: 678 us -> 129 us (0.19)
  the two profiles are of different devices: /device:TPU:6 before, /device:TPU:1 now
where the time goes in v3:
time: 129 us; the launch traced here: 128 us
  Pallas kernels  123 us (95%)
  local copies, waits for them, and re-layouts  3.6 us (3%)
  between operations  1.29 us (1%)
    pallas_call x1, Pallas kernels, on_device(): pl.pallas_call(functools.partial(kernel, share, 1.0 / (rows * NE)), out_s...  123 us
    unnamed x6, local copies, waits for them, and re-layouts  3.6 us

profile of v3, /device:TPU:1, one launch (start us, length us, event | category | flops | bytes accessed | tf_op | source)
XLA Modules:
  0.0 128.0 jit_solution(9241796243576061538)
XLA Ops:
  1.3 0.0 copy-start
  1.3 1.4 %copy-done = bf16[1024,704]{0,1:T(8,128)(2,1)S(1)} copy-done((bf16[1024,704]{0,1:T(8,128)(2,1)S(1)}, bf16[1024,704]{0,1:T(8,128)(2,1)}, u32[]{:S(2)}) %copy-start) | copy-done | bytes 1441816
  2.6 0.0 copy-start.1
  2.6 0.9 copy-done.1
  3.5 123.1 %shard_map.59 = (f32[64,1024]{1,0:T(8,128)S(1)}, f32[22,1024]{1,0:T(8,128)S(1)}) custom-call(bf16[1024,1024]{1,0:T(8,128)(2,1)} %x_ref.1, s32[1]{0:T(128)S(6)} %copy.8.n_ref, bf16[64,1024]{1,0:T(8,128)(2,1)S(1)} %bitcast.3, bf16[704,1024]{1,0:T(8,128)(2,1)S(1)} %bitcast.2), custom_call_target="tpu_custom_call" | custom-call | flops 10737418240 | bytes 8388608 | tf_op jit(solution)/shard_map/pallas_call | solution.py:333
  126.6 0.7 copy.9
  127.3 0.6 copy.10
Async XLA Ops:
  1.3 1.4 %copy-start = (bf16[1024,704]{0,1:T(8,128)(2,1)S(1)}, bf16[1024,704]{0,1:T(8,128)(2,1)}, u32[]{:S(2)}) copy-start(bf16[1024,704]{0,1:T(8,128)(2,1)} %param.7) | copy-start | bytes 4325380
  2.6 0.9 copy-start.1

commit v4 on v3

v4 whole, which is shorter than its diff:
```python
import functools

import jax
import jax.numpy as jnp
from jax import lax
from jax.experimental import pallas as pl
from jax.experimental.pallas import tpu as pltpu
from jax.sharding import PartitionSpec as P

F32, BF16 = jnp.float32, jnp.bfloat16
MESH = pl.DeviceIdType.MESH
N, DIN, B, MB = 1024, 1024, 128, 16
NE, NZ, NQ = 32, 16, 16
SEL = 24
HALF = NQ * SEL


def split(x):
    hi = x.astype(BF16)
    return hi, (x - hi.astype(F32)).astype(BF16)


def dot_nt(a, b):
    return lax.dot_general(a, b, (((1,), (1,)), ((), ())), preferred_element_type=F32)


def dot_nn(a, b):
    return jnp.dot(a, b, preferred_element_type=F32)


def dot_tn(a, b):
    return lax.dot_general(a, b, (((0,), (0,)), ((), ())), preferred_element_type=F32)


def factor(w):
    row = lax.broadcasted_iota(jnp.int32, (MB, B), 0)
    for m in range(B // MB):
        r0 = m * MB
        R = w[r0:r0 + MB, :]
        C = jnp.stack([jnp.broadcast_to(R[:, r0 + t:r0 + t + 1], (MB, B)) for t in range(MB)], axis=0)
        S = jnp.ones((MB, B), F32)
        for j in range(MB):
            c = C[0]
            d = jnp.broadcast_to(c[j:j + 1, :], (MB, B))
            S = jnp.where(row >= j, lax.rsqrt(d), S)
            if j < MB - 1:
                mult = jnp.where(row > j, c * (1.0 / d), 0.0)
                R = R - jnp.concatenate([mult, mult], axis=1) * R[j:j + 1, :]
                C = C[1:] - mult[None] * C[1:, j:j + 1, :]
        U = R * jnp.concatenate([S, S], axis=1)
        w[r0:r0 + MB, :] = U
        if r0 + MB < B:
            hi, lo = split(U)
            lhs = jnp.concatenate([hi[:, :B], hi[:, :B], lo[:, :B]], axis=0)
            rhs = jnp.concatenate([hi, lo, hi], axis=0)
            upd = dot_tn(lhs, rhs)
            w[r0 + MB:, :] = w[r0 + MB:, :] - upd[r0 + MB:, :]


def times_split(hi, lo, b2):
    x = dot_nt(hi, b2)
    return x[:, :B] + x[:, B:] + dot_nt(lo, b2[:B])


def kernel(share, scale, x_ref, n_ref, wp_ref, wr_ref, panel_out, rest_out,
           xs, wr, wt, pf, wrt, rft, pt, part, prec, zb, gb, rsend, rmate, rrecv, w, pan, hi_s, lo_s, tts, xh, xl, loc, sems):
    e, z = lax.axis_index("ex"), lax.axis_index("fac")
    chip, core = e // 2, e % 2
    mate = {"ex": chip * 2 + 1 - core}
    lq, rg, zg = chip // 4, core * 4 + chip % 4, z // 4
    rows, own, wide = xs.shape[0], wp_ref.shape[0], wr_ref.shape[0]
    (s_w, r_w, s_p, r_p, s_m, r_m, s_g, r_g, s_z, r_z, s_a, r_a, s_b, r_b, s_r, r_r, s_h, r_h) = sems

    def z_peer(k):
        return {"fac": (z + k) % NZ}

    def e_peer(k):
        return {"ex": (e + k) % NE}

    def chip_peer(k):
        return {"ex": ((chip + k) % NQ) * 2 + core}

    def each(lo, hi, body):
        def run(k, _):
            body(k)
            return 0
        lax.fori_loop(lo, hi, run, 0)

    def unrolled(lo, hi, body):
        for k in range(lo, hi):
            body(k)

    def blocks(count, span, body):
        each(0, count, lambda i: body(pl.ds(pl.multiple_of(i * span, span), span)))

    def copy(src, dst, send, recv, device):
        return pltpu.make_async_remote_copy(src, dst, send, recv, device_id=device, device_id_type=MESH)

    def arrived(ref, sem):
        pltpu.make_async_copy(ref, ref, sem).wait()

    def lanes(i, count=1):
        return pl.ds(pl.multiple_of(i * 128, 128), 128 * count)

    barrier = pltpu.get_barrier_semaphore()
    unrolled(1, NZ, lambda k: pl.semaphore_signal(barrier, inc=1, device_id=z_peer(k), device_id_type=MESH))
    unrolled(1, NE, lambda k: pl.semaphore_signal(barrier, inc=1, device_id=e_peer(k), device_id_type=MESH))
    own_tile = wp_ref.at[pl.ds(pl.multiple_of(lq * 16, 16), 16), lanes(rg)]
    local = [
        pltpu.make_async_copy(own_tile, wt.at[z, lq, :, lanes(rg)], loc.at[0]),
        pltpu.make_async_copy(x_ref, xs, loc.at[1]),
        pltpu.make_async_copy(wr_ref, wr, loc.at[2]),
        pltpu.make_async_copy(wp_ref, pt, loc.at[3]),
    ]
    for c in local:
        c.start()
    pl.semaphore_wait(barrier, NZ - 1 + NE - 1)

    def z_weight(k):
        return copy(own_tile, wt.at[z, lq, :, lanes(rg)], s_w.at[0], r_w.at[0], z_peer(k))

    unrolled(1, NZ, lambda k: z_weight(k).start())
    local[0].wait()
    arrived(wt.at[pl.ds(0, NZ - 1), lq, :, lanes(rg)], r_w.at[0])

    tile = wt.at[:, lq, :, lanes(rg)]
    unrolled(1, NQ, lambda k: copy(tile, tile, s_p.at[0], r_p.at[lq], chip_peer(k)).start())

    def pass_weight(y):
        piece = wt.at[:, y, :, lanes(core * 4, 4)]
        copy(piece, piece, s_m.at[y], r_m.at[y], mate).start()

    for c in local[1:]:
        c.wait()

    def mask(at):
        live = lax.broadcasted_iota(jnp.int32, (256, 1), 0) + at.start < n_ref[0]
        xs[at, :] = jnp.where(live, xs[at, :].astype(F32), 0.0).astype(BF16)

    blocks(rows // 256, 256, mask)

    def select(at):
        c = (lax.broadcasted_iota(jnp.int32, (128, 1), 0) + at.start).astype(F32)
        b = jnp.floor((c + 0.5) * (1.0 / SEL))
        t = c - SEL * b
        device = jnp.where(b < NQ, 2 * b, 2 * (b - NQ) + 1)
        want = jnp.where(t < share, device * share + t, -1.0)
        sel = (lax.broadcasted_iota(jnp.int32, (128, wide), 1).astype(F32) == want).astype(BF16)
        wrt[at, :] = dot_nn(sel, wr[...]).astype(BF16)

    blocks(NE * SEL // 128, 128, select)

    def rest_features(at):
        rft[at, :] = jnp.maximum(dot_nt(wrt[at, :], xs[...]), 0.0).astype(BF16)

    blocks(NE * SEL // 256, 256, rest_features)
    pt[...] = jnp.maximum(dot_nt(pt[...], xs[...]), 0.0).astype(BF16)

    for y in range(4):
        pl.when(lq == y)(lambda: arrived(wt.at[:, y, :, lanes(core * 4, 3)], r_p.at[y]))
        pl.when(lq != y)(lambda: arrived(wt.at[:, y, :, lanes(core * 4, 4)], r_p.at[y]))
        pass_weight(y)
    for y in range(4):
        arrived(wt.at[:, y, :, lanes(4 - core * 4, 4)], r_m.at[y])

    def panel_features(at):
        pf[at, :] = jnp.maximum(dot_nt(xs[at, :], wt[...].reshape(N, DIN)), 0.0).astype(BF16)

    blocks(rows // 256, 256, panel_features)

    mine = dot_nn(pt[...], pf[...])
    for lt in range(8):
        part[lt // 4, lt % 4] = mine[:, lt * 128:lt * 128 + 128].reshape(8, 8, 128)

    def gram_part(k):
        i = (e + k) % NE
        piece = part.at[:, (i // 8 + 4 - zg) % 4, (i % 2) * 4 + (i // 2) % 4]
        return copy(piece, prec.at[k], s_g.at[0], r_g.at[0], e_peer(k))

    unrolled(1, NE, lambda k: gram_part(k).start())

    def rest_gram(c):
        at = pl.ds(pl.multiple_of(c * HALF, HALF), HALF)
        rsend[c] = dot_nn(rft[at, :], pf[...]).reshape(NQ, SEL, N)

    rest_half = copy(rsend.at[1 - core], rmate, s_h.at[0], r_h.at[0], mate)
    rest_gram(1 - core)
    rest_half.start()
    arrived(prec.at[pl.ds(1, NE - 1)], r_g.at[0])
    total = part[:, (lq + 4 - zg) % 4, rg]
    for k in range(1, NE):
        total = total + prec[k]
    zb[:, z] = total
    unrolled(1, NZ, lambda k: copy(zb.at[:, z], zb.at[:, z], s_z.at[0], r_z.at[0], z_peer(k)).start())
    rest_gram(core)
    arrived(zb.at[:, pl.ds(0, NZ - 1)], r_z.at[0])

    parts = (pl.ds(0, 1), pl.ds(1, 3), pl.ds(4, 2))
    for p in range(4):
        gb[core, chip, p] = zb[0, pl.ds(((lq + 4 - p) % 4) * 4, 4)]
    gb[core, chip, 4:] = zb[1, 8:].reshape(2, 4, 8, 128)

    def send_panels(i):
        piece = gb.at[core, chip, parts[i]]
        unrolled(1, NQ, lambda k: copy(piece, piece, s_a.at[i], r_a.at[i], chip_peer(k)).start())

    def pass_panels(i):
        arrived(gb.at[core, pl.ds(0, NQ - 1), parts[i]], r_a.at[i])
        piece = gb.at[core, :, parts[i]]
        copy(piece, piece, s_b.at[i], r_b.at[i], mate).start()

    def wait_panels(i):
        arrived(gb.at[1 - core, :, parts[i]], r_b.at[i])

    def panel(c):
        tiles = []
        for zz in range(2 * c, NZ):
            q = (c + zz // 4) % 4
            slot = c if c < 4 else 4 + zz // 4 - 2
            tiles += [gb[i // 4, q * 4 + i % 4, slot, zz % 4] for i in range(8)]
        return jnp.concatenate(tiles, axis=0)

    send_panels(0)
    send_panels(1)
    send_panels(2)

    rest_half.wait_recv()

    def add_mate(i):
        rsend[core, i] = rsend[core, i] + rmate[i]

    each(0, NQ, add_mate)
    unrolled(1, NQ, lambda k: copy(rsend.at[core, (chip + k) % NQ], rrecv.at[k], s_r.at[0], r_r.at[0], chip_peer(k)).start())

    ri = lax.broadcasted_iota(jnp.int32, (B, B), 0)
    ci = lax.broadcasted_iota(jnp.int32, (B, B), 1)
    eye = (ri == ci).astype(F32)

    def step(j):
        for c in range(N // B):
            @pl.when(j == c)
            def _():
                r0 = c * B
                if c == 0:
                    pass_panels(0)
                if c in (0, 1, 4):
                    wait_panels((0, 1, 4).index(c))
                a = panel(c) * scale
                a = jnp.concatenate([a[:B] + eye] + ([a[B:]] if r0 + B < N else []), axis=0)
                if c:
                    b2 = jnp.concatenate([hi_s[r0:r0 + B, :r0], lo_s[r0:r0 + B, :r0]], axis=0)
                    a = a - times_split(hi_s[r0:, :r0], lo_s[r0:, :r0], b2)
                pan[r0:, :] = a
                w[:, :B] = a[:B, :]
                w[:, B:] = eye

                if c in (0, 2):
                    pass_panels(1 + c // 2)

        factor(w)
        for c in range(N // B):
            @pl.when(j == c)
            def _():
                r0 = c * B
                t2 = jnp.concatenate(split(w[:, B:]), axis=0)
                tts[c] = t2
                ah, al = split(pan[r0:, :])
                lp = times_split(ah, al, t2)
                lp = jnp.concatenate([jnp.where(ri >= ci, lp[:B], 0.0)] + ([lp[B:]] if r0 + B < N else []), axis=0)
                h, l = split(lp)
                hi_s[r0:, r0:r0 + B] = h
                lo_s[r0:, r0:r0 + B] = l
                pan[r0:, :] = lp
                ours = pan[pl.ds(pl.multiple_of(z * own, own), own), :]
                panel_out[:, r0:r0 + B] = jnp.where(z >= 2 * c, ours, 0.0)

    each(0, N // B, step)

    arrived(rrecv.at[pl.ds(1, NQ - 1)], r_r.at[0])
    total = lax.fori_loop(1, NQ, lambda k, t: t + rrecv[k], rsend[core, chip]) * scale
    for c in range(N // B):
        r0 = c * B
        a = total[:, r0:r0 + B]
        if c:
            b2 = jnp.concatenate([hi_s[r0:r0 + B, :r0], lo_s[r0:r0 + B, :r0]], axis=0)
            a = a - times_split(xh[:SEL, :r0], xl[:SEL, :r0], b2)
        ah, al = split(a)
        a = times_split(ah, al, tts[c])
        rest_out[:, r0:r0 + B] = a[:share]
        h, l = split(a)
        xh[:SEL, r0:r0 + B] = h
        xl[:SEL, r0:r0 + B] = l

    arrived(wt.at[pl.ds(0, NZ - 1), lq, :, lanes(rg)], s_w.at[0])
    arrived(wt.at[:, 0:3, :, lanes(0, 5)], s_p.at[0])
    for y in range(4):
        arrived(wt.at[:, y, :, lanes(core * 4, 4)], s_m.at[y])
    arrived(prec.at[pl.ds(1, NE - 1)], s_g.at[0])
    arrived(zb.at[:, pl.ds(0, NZ - 1)], s_z.at[0])
    rest_half.wait_send()
    arrived(rrecv.at[pl.ds(1, NQ - 1)], s_r.at[0])
    for i in range(3):
        arrived(gb.at[core, pl.ds(0, NQ - 1), parts[i]], s_a.at[i])
        arrived(gb.at[core, :, parts[i]], s_b.at[i])


def on_device(samples, counts, panel_weight, rest_weight):
    rows = samples.shape[0]
    own, wide = panel_weight.shape[1], rest_weight.shape[1]
    share = wide // NE
    vmem, anywhere = pl.BlockSpec(memory_space=pltpu.VMEM), pl.BlockSpec(memory_space=pltpu.HBM)
    counted = [1, 1, 1, 4, 4, 4, 1, 1, 1, 1, 3, 3, 3, 3, 1, 1, 1, 1]
    return pl.pallas_call(
        functools.partial(kernel, share, 1.0 / (rows * NE)),
        out_shape=(jax.ShapeDtypeStruct((own, N), F32), jax.ShapeDtypeStruct((share, N), F32)),
        in_specs=[anywhere, pl.BlockSpec(memory_space=pltpu.SMEM), anywhere, anywhere],
        out_specs=(vmem, vmem),
        scratch_shapes=[
            pltpu.VMEM((rows, DIN), BF16),
            pltpu.VMEM((wide, DIN), BF16),
            pltpu.VMEM((NZ, 4, 16, DIN), BF16),
            pltpu.VMEM((rows, N), BF16),
            pltpu.VMEM((NE * SEL, DIN), BF16),
            pltpu.VMEM((NE * SEL, rows), BF16),
            pltpu.VMEM((own, rows), BF16),
            pltpu.VMEM((2, 4, 8, 8, 128), F32),
            pltpu.VMEM((NE, 2, 8, 128), F32),
            pltpu.VMEM((2, NZ, 8, 128), F32),
            pltpu.VMEM((2, NQ, 6, 4, 8, 128), F32),
            pltpu.VMEM((2, NQ, SEL, N), F32),
            pltpu.VMEM((NQ, SEL, N), F32),
            pltpu.VMEM((NQ, SEL, N), F32),
            pltpu.VMEM((B, 2 * B), F32),
            pltpu.VMEM((N, B), F32),
            pltpu.VMEM((N, N), BF16),
            pltpu.VMEM((N, N), BF16),
            pltpu.VMEM((8, 2 * B, B), BF16),
            pltpu.VMEM((32, N), BF16),
            pltpu.VMEM((32, N), BF16),
            pltpu.SemaphoreType.DMA((4,)),
            [pltpu.SemaphoreType.DMA((c,)) for c in counted],
        ],
        compiler_params=pltpu.CompilerParams(
            collective_id=0, has_side_effects=True, vmem_limit_bytes=60 * 2**20
        ),
        cost_estimate=pl.CostEstimate(flops=10 * 2**30, bytes_accessed=8 * 2**20, transcendentals=0),
    )(samples, counts, panel_weight.T, rest_weight.T)


def solution(mesh):
    in_specs = (P("ex", None), P("ex"), P(None, "fac"), P(None, "fac"))
    out_specs = (P("fac", None), P(("fac", "ex"), None))
    return jax.shard_map(
        on_device, mesh=mesh, in_specs=in_specs, out_specs=out_specs, check_vma=False
    )
```

time: 129 us -> 124 us (0.961)
  the two profiles are of different devices: /device:TPU:1 before, /device:TPU:2 now
where the time goes in v4:
time: 124 us
  Pallas kernels  119 us (96%)
  local copies, waits for them, and re-layouts  3.21 us (3%)
  between operations  1.28 us (1%)
    pallas_call x1, Pallas kernels, on_device(): pl.pallas_call(functools.partial(kernel, share, 1.0 / (rows * NE)), out_s...  119 us
    unnamed x2, local copies, waits for them, and re-layouts  3.21 us

profile of v4, /device:TPU:2, one launch (start us, length us, event | category | flops | bytes accessed | tf_op | source)
XLA Modules:
  0.0 123.6 jit_solution(5861551352038154459)
XLA Ops:
  1.3 119.1 %shard_map.59 = (f32[64,1024]{1,0:T(8,128)}, f32[22,1024]{1,0:T(8,128)}) custom-call(bf16[1024,1024]{1,0:T(8,128)(2,1)} %x_ref.1, s32[1]{0:T(128)S(6)} %copy.8.n_ref, bf16[64,1024]{1,0:T(8,128)(2,1)} %bitcast.3, bf16[704,1024]{1,0:T(8,128)(2,1)} %bitcast.2), custom_call_target="tpu_custom_call" | custom-call | flops 10737418240 | bytes 8388608 | tf_op jit(solution)/shard_map/pallas_call | solution.py:313
  120.4 1.7 %copy.9 = f32[64,1024]{1,0:T(8,128)} copy(f32[64,1024]{1,0:T(8,128)} %get-tuple-element.4) | data formatting | bytes 524288
  122.1 1.5 %copy.10 = f32[22,1024]{1,0:T(8,128)} copy(f32[22,1024]{1,0:T(8,128)} %get-tuple-element.5) | data formatting | bytes 180224

commit v5 on v4

--- a/solution.py
+++ b/solution.py
@@ -13,6 +13,8 @@
 NE, NZ, NQ = 32, 16, 16
 SEL = 24
 HALF = NQ * SEL
+FIRST = (0, 1, 2, 4)
+REST_FROM = 7
 
 
 def split(x):
@@ -32,38 +34,114 @@
     return lax.dot_general(a, b, (((0,), (0,)), ((), ())), preferred_element_type=F32)
 
 
-def factor(w):
+def times_split(hi, lo, b2):
+    x = dot_nt(hi, b2)
+    return x[:, :B] + x[:, B:] + dot_nt(lo, b2[:B])
+
+
+def factor(w, beside):
     row = lax.broadcasted_iota(jnp.int32, (MB, B), 0)
-    for m in range(B // MB):
+    parts = B // MB
+    R = w[:MB, :]
+    for m in range(parts):
         r0 = m * MB
-        R = w[r0:r0 + MB, :]
+        G = R
         C = jnp.stack([jnp.broadcast_to(R[:, r0 + t:r0 + t + 1], (MB, B)) for t in range(MB)], axis=0)
+        last = m == parts - 1
+        if not last:
+            low = w[r0 + MB:, :]
+            ah, al = split(low[:, r0:r0 + MB])
+            lhs = jnp.concatenate([ah, al, ah], axis=1)
         S = jnp.ones((MB, B), F32)
+        V = jnp.ones((MB, B), F32)
         for j in range(MB):
             c = C[0]
             d = jnp.broadcast_to(c[j:j + 1, :], (MB, B))
+            inv = 1.0 / d
             S = jnp.where(row >= j, lax.rsqrt(d), S)
+            V = jnp.where(row >= j, inv, V)
+            mult = jnp.where(row != j, c * inv, 0.0)
             if j < MB - 1:
-                mult = jnp.where(row > j, c * (1.0 / d), 0.0)
-                R = R - jnp.concatenate([mult, mult], axis=1) * R[j:j + 1, :]
+                down = jnp.where(row > j, mult, 0.0)
+                R = R - jnp.concatenate([down, down], axis=1) * R[j:j + 1, :]
                 C = C[1:] - mult[None] * C[1:, j:j + 1, :]
+            G = G - jnp.concatenate([mult, mult], axis=1) * G[j:j + 1, :]
         U = R * jnp.concatenate([S, S], axis=1)
+        if not last:
+            zh, zl = split(G * jnp.concatenate([V, V], axis=1))
+            rhs = jnp.concatenate([zh, zh, zl], axis=0)
+            rest = low - jnp.dot(lhs, rhs, preferred_element_type=F32)
+            R = rest[:MB]
+            w[r0 + MB:, :] = rest
         w[r0:r0 + MB, :] = U
-        if r0 + MB < B:
-            hi, lo = split(U)
-            lhs = jnp.concatenate([hi[:, :B], hi[:, :B], lo[:, :B]], axis=0)
-            rhs = jnp.concatenate([hi, lo, hi], axis=0)
-            upd = dot_tn(lhs, rhs)
-            w[r0 + MB:, :] = w[r0 + MB:, :] - upd[r0 + MB:, :]
-
-
-def times_split(hi, lo, b2):
-    x = dot_nt(hi, b2)
-    return x[:, :B] + x[:, B:] + dot_nt(lo, b2[:B])
+        for f in beside[len(beside) * m // parts:len(beside) * (m + 1) // parts]:
+            f()
+
+
+def cholesky(gram, w, tts, hi_s, lo_s, p_hi, p_lo, dn, extra, before):
+    ri = lax.broadcasted_iota(jnp.int32, (B, B), 0)
+    ci = lax.broadcasted_iota(jnp.int32, (B, B), 1)
+    eye = (ri == ci).astype(F32)
+    nb = N // B
+    def rows_of(c):
+        return jnp.concatenate([hi_s[c * B:c * B + B, :c * B], lo_s[c * B:c * B + B, :c * B]], axis=0)
+
+    def store(r0, r1, c, x):
+        h, l = split(x)
+        hi_s[r0:r1, c * B:c * B + B] = h
+        lo_s[r0:r1, c * B:c * B + B] = l
+
+    def solved(r0, r1, c):
+        store(r0, r1, c, times_split(p_hi[c % 2, r0:r1, :], p_lo[c % 2, r0:r1, :], tts[c]))
+
+    def updated(r0, r1, c):
+        a = gram(c, r0, r1)
+        if c:
+            a = a - times_split(hi_s[r0:r1, :c * B], lo_s[r0:r1, :c * B], rows_of(c))
+        h, l = split(a)
+        p_hi[c % 2, r0:r1, :] = h
+        p_lo[c % 2, r0:r1, :] = l
+
+    def next_diag(c):
+        k = (c - 1) * B
+        r0 = c * B
+        a = gram(c, r0, r0 + B) + eye
+        if k:
+            b2 = jnp.concatenate([hi_s[r0:r0 + B, :k], lo_s[r0:r0 + B, :k]], axis=0)
+            a = a - times_split(hi_s[r0:r0 + B, :k], lo_s[r0:r0 + B, :k], b2)
+        dn[...] = a
+
+    before(0)
+    d = gram(0, 0, B) + eye
+    for c in range(nb):
+        r0 = c * B
+        wc = w.at[c % 2]
+        wc[:, :B] = d
+        wc[:, B:] = eye
+        work = extra(c)
+        if c + 1 < nb:
+            for r in [(r0 + B, r0 + 2 * B)] + [(i, min(i + 2 * B, N)) for i in range(r0 + 2 * B, N, 2 * B)]:
+                if c:
+                    work.append(functools.partial(solved, *r, c - 1))
+                work.append(functools.partial(updated, *r, c))
+            work.append(functools.partial(before, c + 1))
+            work.append(functools.partial(next_diag, c + 1))
+        factor(wc, work)
+        t2 = jnp.concatenate(split(wc[:, B:]), axis=0)
+        tts[c] = t2
+        u = jnp.where(ri <= ci, wc[:, :B], 0.0)
+        store(r0, r0 + B, c, u.T)
+        if c + 1 < nb:
+            x = times_split(p_hi[c % 2, r0 + B:r0 + 2 * B, :], p_lo[c % 2, r0 + B:r0 + 2 * B, :], t2)
+            h, l = split(x)
+            hi_s[r0 + B:r0 + 2 * B, r0:r0 + B] = h
+            lo_s[r0 + B:r0 + 2 * B, r0:r0 + B] = l
+            d = dn[...] - times_split(h, l, jnp.concatenate([h, l], axis=0))
 
 
 def kernel(share, scale, x_ref, n_ref, wp_ref, wr_ref, panel_out, rest_out,
-           xs, wr, wt, pf, wrt, rft, pt, part, prec, zb, gb, rsend, rmate, rrecv, w, pan, hi_s, lo_s, tts, xh, xl, loc, sems):
+           xs, wr, wt, pf, wrt, rft, pt, part, prec, zb, gb, rsend, rmate, rrecv, rtot, ra,
+           w, hi_s, lo_s, p_hi, p_lo, dn, tts, xh, xl, loc, sems):
     e, z = lax.axis_index("ex"), lax.axis_index("fac")
     chip, core = e // 2, e % 2
     mate = {"ex": chip * 2 + 1 - core}
@@ -195,7 +273,7 @@
     rest_gram(core)
     arrived(zb.at[:, pl.ds(0, NZ - 1)], r_z.at[0])
 
-    parts = (pl.ds(0, 1), pl.ds(1, 3), pl.ds(4, 2))
+    parts = (pl.ds(0, 1), pl.ds(1, 1), pl.ds(2, 2), pl.ds(4, 2))
     for p in range(4):
         gb[core, chip, p] = zb[0, pl.ds(((lq + 4 - p) % 4) * 4, 4)]
     gb[core, chip, 4:] = zb[1, 8:].reshape(2, 4, 8, 128)
@@ -212,17 +290,16 @@
     def wait_panels(i):
         arrived(gb.at[1 - core, :, parts[i]], r_b.at[i])
 
-    def panel(c):
+    def panel(c, r0, r1):
         tiles = []
-        for zz in range(2 * c, NZ):
+        for zz in range(r0 // 64, r1 // 64):
             q = (c + zz // 4) % 4
             slot = c if c < 4 else 4 + zz // 4 - 2
             tiles += [gb[i // 4, q * 4 + i % 4, slot, zz % 4] for i in range(8)]
         return jnp.concatenate(tiles, axis=0)
 
-    send_panels(0)
-    send_panels(1)
-    send_panels(2)
+    for i in range(4):
+        send_panels(i)
 
     rest_half.wait_recv()
 
@@ -232,64 +309,51 @@
     each(0, NQ, add_mate)
     unrolled(1, NQ, lambda k: copy(rsend.at[core, (chip + k) % NQ], rrecv.at[k], s_r.at[0], r_r.at[0], chip_peer(k)).start())
 
-    ri = lax.broadcasted_iota(jnp.int32, (B, B), 0)
-    ci = lax.broadcasted_iota(jnp.int32, (B, B), 1)
-    eye = (ri == ci).astype(F32)
-
-    def step(j):
-        for c in range(N // B):
-            @pl.when(j == c)
-            def _():
-                r0 = c * B
-                if c == 0:
-                    pass_panels(0)
-                if c in (0, 1, 4):
-                    wait_panels((0, 1, 4).index(c))
-                a = panel(c) * scale
-                a = jnp.concatenate([a[:B] + eye] + ([a[B:]] if r0 + B < N else []), axis=0)
-                if c:
-                    b2 = jnp.concatenate([hi_s[r0:r0 + B, :r0], lo_s[r0:r0 + B, :r0]], axis=0)
-                    a = a - times_split(hi_s[r0:, :r0], lo_s[r0:, :r0], b2)
-                pan[r0:, :] = a
-                w[:, :B] = a[:B, :]
-                w[:, B:] = eye
-
-                if c in (0, 2):
-                    pass_panels(1 + c // 2)
-
-        factor(w)
-        for c in range(N // B):
-            @pl.when(j == c)
-            def _():
-                r0 = c * B
-                t2 = jnp.concatenate(split(w[:, B:]), axis=0)
-                tts[c] = t2
-                ah, al = split(pan[r0:, :])
-                lp = times_split(ah, al, t2)
-                lp = jnp.concatenate([jnp.where(ri >= ci, lp[:B], 0.0)] + ([lp[B:]] if r0 + B < N else []), axis=0)
-                h, l = split(lp)
-                hi_s[r0:, r0:r0 + B] = h
-                lo_s[r0:, r0:r0 + B] = l
-                pan[r0:, :] = lp
-                ours = pan[pl.ds(pl.multiple_of(z * own, own), own), :]
-                panel_out[:, r0:r0 + B] = jnp.where(z >= 2 * c, ours, 0.0)
-
-    each(0, N // B, step)
-
-    arrived(rrecv.at[pl.ds(1, NQ - 1)], r_r.at[0])
-    total = lax.fori_loop(1, NQ, lambda k, t: t + rrecv[k], rsend[core, chip]) * scale
-    for c in range(N // B):
+    def rest_ready():
+        arrived(rrecv.at[pl.ds(1, NQ - 1)], r_r.at[0])
+        rtot[...] = lax.fori_loop(1, NQ, lambda k, t: t + rrecv[k], rsend[core, chip]) * scale
+
+    def rest_update(c):
         r0 = c * B
-        a = total[:, r0:r0 + B]
+        a = rtot[:, r0:r0 + B]
         if c:
             b2 = jnp.concatenate([hi_s[r0:r0 + B, :r0], lo_s[r0:r0 + B, :r0]], axis=0)
             a = a - times_split(xh[:SEL, :r0], xl[:SEL, :r0], b2)
-        ah, al = split(a)
-        a = times_split(ah, al, tts[c])
+        ra[...] = a
+
+    def rest_solve(c):
+        r0 = c * B
+        a = times_split(*split(ra[...]), tts[c])
         rest_out[:, r0:r0 + B] = a[:share]
         h, l = split(a)
         xh[:SEL, r0:r0 + B] = h
         xl[:SEL, r0:r0 + B] = l
+
+    def beside(c):
+        work = []
+        if c in (1, 2):
+            work.append(lambda: pass_panels(c + 1))
+        if c == REST_FROM:
+            work.append(rest_ready)
+            for k in range(c):
+                work += [functools.partial(rest_update, k), functools.partial(rest_solve, k)]
+        elif c > REST_FROM:
+            work.append(lambda: rest_solve(c - 1))
+        if c >= REST_FROM:
+            work.append(lambda: rest_update(c))
+        return work
+
+    def before(c):
+        if c < 2:
+            pass_panels(c)
+        if c in FIRST:
+            wait_panels(FIRST.index(c))
+
+    cholesky(lambda c, r0, r1: panel(c, r0, r1) * scale, w, tts, hi_s, lo_s, p_hi, p_lo, dn, beside, before)
+    rest_solve(N // B - 1)
+    ours = pl.ds(pl.multiple_of(z * own, own), own)
+    below = lax.broadcasted_iota(jnp.int32, (own, N), 1) <= lax.broadcasted_iota(jnp.int32, (own, N), 0) + z * own
+    panel_out[...] = jnp.where(below, hi_s[ours, :].astype(F32) + lo_s[ours, :].astype(F32), 0.0)
 
     arrived(wt.at[pl.ds(0, NZ - 1), lq, :, lanes(rg)], s_w.at[0])
     arrived(wt.at[:, 0:3, :, lanes(0, 5)], s_p.at[0])
@@ -299,7 +363,7 @@
     arrived(zb.at[:, pl.ds(0, NZ - 1)], s_z.at[0])
     rest_half.wait_send()
     arrived(rrecv.at[pl.ds(1, NQ - 1)], s_r.at[0])
-    for i in range(3):
+    for i in range(4):
         arrived(gb.at[core, pl.ds(0, NQ - 1), parts[i]], s_a.at[i])
         arrived(gb.at[core, :, parts[i]], s_b.at[i])
 
@@ -309,7 +373,7 @@
     own, wide = panel_weight.shape[1], rest_weight.shape[1]
     share = wide // NE
     vmem, anywhere = pl.BlockSpec(memory_space=pltpu.VMEM), pl.BlockSpec(memory_space=pltpu.HBM)
-    counted = [1, 1, 1, 4, 4, 4, 1, 1, 1, 1, 3, 3, 3, 3, 1, 1, 1, 1]
+    counted = [1, 1, 1, 4, 4, 4, 1, 1, 1, 1, 4, 4, 4, 4, 1, 1, 1, 1]
     return pl.pallas_call(
         functools.partial(kernel, share, 1.0 / (rows * NE)),
         out_shape=(jax.ShapeDtypeStruct((own, N), F32), jax.ShapeDtypeStruct((share, N), F32)),
@@ -330,10 +394,14 @@
             pltpu.VMEM((2, NQ, SEL, N), F32),
             pltpu.VMEM((NQ, SEL, N), F32),
             pltpu.VMEM((NQ, SEL, N), F32),
-            pltpu.VMEM((B, 2 * B), F32),
-            pltpu.VMEM((N, B), F32),
+            pltpu.VMEM((SEL, N), F32),
+            pltpu.VMEM((SEL, B), F32),
+            pltpu.VMEM((2, B, 2 * B), F32),
             pltpu.VMEM((N, N), BF16),
             pltpu.VMEM((N, N), BF16),
+            pltpu.VMEM((2, N, B), BF16),
+            pltpu.VMEM((2, N, B), BF16),
+            pltpu.VMEM((B, B), F32),
             pltpu.VMEM((8, 2 * B, B), BF16),
             pltpu.VMEM((32, N), BF16),
             pltpu.VMEM((32, N), BF16),

time: 124 us -> 118 us (0.952)
  the two profiles are of different devices: /device:TPU:2 before, /device:TPU:1 now
where the time goes in v5:
time: 118 us; the launch traced here: 117 us
  Pallas kernels  112 us (95%)
  local copies, waits for them, and re-layouts  3.21 us (3%)
  between operations  1.28 us (1%)
    pallas_call x1, Pallas kernels, on_device(): pl.pallas_call(functools.partial(kernel, share, 1.0 / (rows * NE)), out_s...  112 us
    unnamed x2, local copies, waits for them, and re-layouts  3.21 us

profile of v5, /device:TPU:1, one launch (start us, length us, event | category | flops | bytes accessed | tf_op | source)
XLA Modules:
  0.0 116.7 jit_solution(13296155374408546970)
XLA Ops:
  1.3 112.2 %shard_map.59 = (f32[64,1024]{1,0:T(8,128)}, f32[22,1024]{1,0:T(8,128)}) custom-call(bf16[1024,1024]{1,0:T(8,128)(2,1)} %x_ref.1, s32[1]{0:T(128)S(6)} %copy.8.n_ref, bf16[64,1024]{1,0:T(8,128)(2,1)} %bitcast.3, bf16[704,1024]{1,0:T(8,128)(2,1)} %bitcast.2), custom_call_target="tpu_custom_call" | custom-call | flops 10737418240 | bytes 8388608 | tf_op jit(solution)/shard_map/pallas_call | solution.py:377
  113.5 1.7 %copy.9 = f32[64,1024]{1,0:T(8,128)} copy(f32[64,1024]{1,0:T(8,128)} %get-tuple-element.4) | data formatting | bytes 524288
  115.1 1.5 %copy.10 = f32[22,1024]{1,0:T(8,128)} copy(f32[22,1024]{1,0:T(8,128)} %get-tuple-element.5) | data formatting | bytes 180224

commit v6 on v5

--- a/solution.py
+++ b/solution.py
@@ -13,7 +13,8 @@
 NE, NZ, NQ = 32, 16, 16
 SEL = 24
 HALF = NQ * SEL
-FIRST = (0, 1, 2, 4)
+FIRST = (0, 1, 2, 3, 4)
+EARLY = 512
 REST_FROM = 7
 
 
@@ -264,16 +265,31 @@
     rest_half = copy(rsend.at[1 - core], rmate, s_h.at[0], r_h.at[0], mate)
     rest_gram(1 - core)
     rest_half.start()
+    rest_gram(core)
     arrived(prec.at[pl.ds(1, NE - 1)], r_g.at[0])
     total = part[:, (lq + 4 - zg) % 4, rg]
     for k in range(1, NE):
         total = total + prec[k]
     zb[:, z] = total
     unrolled(1, NZ, lambda k: copy(zb.at[:, z], zb.at[:, z], s_z.at[0], r_z.at[0], z_peer(k)).start())
-    rest_gram(core)
+
+    rest_half.wait_recv()
+
+    def add_mate(i):
+        rsend[core, i] = rsend[core, i] + rmate[i]
+
+    each(0, NQ, add_mate)
+    columns = (pl.ds(0, EARLY), pl.ds(EARLY, N - EARLY))
+
+    def send_rest(h):
+        unrolled(1, NQ, lambda k: copy(
+            rsend.at[core, (chip + k) % NQ, :, columns[h]], rrecv.at[k, :, columns[h]], s_r.at[h], r_r.at[h], chip_peer(k)
+        ).start())
+
+    send_rest(0)
     arrived(zb.at[:, pl.ds(0, NZ - 1)], r_z.at[0])
 
-    parts = (pl.ds(0, 1), pl.ds(1, 1), pl.ds(2, 2), pl.ds(4, 2))
+    parts = (pl.ds(0, 1), pl.ds(1, 1), pl.ds(2, 1), pl.ds(3, 1), pl.ds(4, 2))
     for p in range(4):
         gb[core, chip, p] = zb[0, pl.ds(((lq + 4 - p) % 4) * 4, 4)]
     gb[core, chip, 4:] = zb[1, 8:].reshape(2, 4, 8, 128)
@@ -298,19 +314,14 @@
             tiles += [gb[i // 4, q * 4 + i % 4, slot, zz % 4] for i in range(8)]
         return jnp.concatenate(tiles, axis=0)
 
-    for i in range(4):
+    for i in range(5):
         send_panels(i)
 
-    rest_half.wait_recv()
-
-    def add_mate(i):
-        rsend[core, i] = rsend[core, i] + rmate[i]
-
-    each(0, NQ, add_mate)
-    unrolled(1, NQ, lambda k: copy(rsend.at[core, (chip + k) % NQ], rrecv.at[k], s_r.at[0], r_r.at[0], chip_peer(k)).start())
+    send_rest(1)
 
     def rest_ready():
-        arrived(rrecv.at[pl.ds(1, NQ - 1)], r_r.at[0])
+        for h in range(2):
+            arrived(rrecv.at[pl.ds(1, NQ - 1), :, columns[h]], r_r.at[h])
         rtot[...] = lax.fori_loop(1, NQ, lambda k, t: t + rrecv[k], rsend[core, chip]) * scale
 
     def rest_update(c):
@@ -331,7 +342,7 @@
 
     def beside(c):
         work = []
-        if c in (1, 2):
+        if c in (1, 2, 3):
             work.append(lambda: pass_panels(c + 1))
         if c == REST_FROM:
             work.append(rest_ready)
@@ -362,8 +373,9 @@
     arrived(prec.at[pl.ds(1, NE - 1)], s_g.at[0])
     arrived(zb.at[:, pl.ds(0, NZ - 1)], s_z.at[0])
     rest_half.wait_send()
-    arrived(rrecv.at[pl.ds(1, NQ - 1)], s_r.at[0])
-    for i in range(4):
+    for h in range(2):
+        arrived(rrecv.at[pl.ds(1, NQ - 1), :, columns[h]], s_r.at[h])
+    for i in range(5):
         arrived(gb.at[core, pl.ds(0, NQ - 1), parts[i]], s_a.at[i])
         arrived(gb.at[core, :, parts[i]], s_b.at[i])
 
@@ -373,7 +385,7 @@
     own, wide = panel_weight.shape[1], rest_weight.shape[1]
     share = wide // NE
     vmem, anywhere = pl.BlockSpec(memory_space=pltpu.VMEM), pl.BlockSpec(memory_space=pltpu.HBM)
-    counted = [1, 1, 1, 4, 4, 4, 1, 1, 1, 1, 4, 4, 4, 4, 1, 1, 1, 1]
+    counted = [1, 1, 1, 4, 4, 4, 1, 1, 1, 1, 5, 5, 5, 5, 2, 2, 1, 1]
     return pl.pallas_call(
         functools.partial(kernel, share, 1.0 / (rows * NE)),
         out_shape=(jax.ShapeDtypeStruct((own, N), F32), jax.ShapeDtypeStruct((share, N), F32)),

time: 118 us -> 110 us (0.932)
  Pallas kernels: 112 us -> 105 us
    pallas_call x1, Pallas kernels: 112 us -> 105 us  [on_device(): pl.pallas_call(functools.partial(kernel, share, 1.0 / (rows * NE)), out_s...]
where the time goes in v6:
time: 110 us
  Pallas kernels  105 us (95%)
  local copies, waits for them, and re-layouts  3.21 us (3%)
  between operations  1.28 us (1%)
    pallas_call x1, Pallas kernels, on_device(): pl.pallas_call(functools.partial(kernel, share, 1.0 / (rows * NE)), out_s...  105 us
    unnamed x2, local copies, waits for them, and re-layouts  3.21 us

profile of v6, /device:TPU:1, one launch (start us, length us, event | category | flops | bytes accessed | tf_op | source)
XLA Modules:
  0.0 109.9 jit_solution(11536210649333296388)
XLA Ops:
  1.3 105.4 %shard_map.59 = (f32[64,1024]{1,0:T(8,128)}, f32[22,1024]{1,0:T(8,128)}) custom-call(bf16[1024,1024]{1,0:T(8,128)(2,1)} %x_ref.1, s32[1]{0:T(128)S(6)} %copy.8.n_ref, bf16[64,1024]{1,0:T(8,128)(2,1)} %bitcast.3, bf16[704,1024]{1,0:T(8,128)(2,1)} %bitcast.2), custom_call_target="tpu_custom_call" | custom-call | flops 10737418240 | bytes 8388608 | tf_op jit(solution)/shard_map/pallas_call | solution.py:389
  106.6 1.7 %copy.9 = f32[64,1024]{1,0:T(8,128)} copy(f32[64,1024]{1,0:T(8,128)} %get-tuple-element.4) | data formatting | bytes 524288
  108.3 1.5 %copy.10 = f32[22,1024]{1,0:T(8,128)} copy(f32[22,1024]{1,0:T(8,128)} %get-tuple-element.5) | data formatting | bytes 180224

commit v7 on v6

--- a/solution.py
+++ b/solution.py
@@ -13,7 +13,6 @@
 NE, NZ, NQ = 32, 16, 16
 SEL = 24
 HALF = NQ * SEL
-FIRST = (0, 1, 2, 3, 4)
 EARLY = 512
 REST_FROM = 7
 
@@ -191,14 +190,15 @@
         pltpu.make_async_copy(wr_ref, wr, loc.at[2]),
         pltpu.make_async_copy(wp_ref, pt, loc.at[3]),
     ]
-    for c in local:
-        c.start()
+    local[0].start()
     pl.semaphore_wait(barrier, NZ - 1 + NE - 1)
 
     def z_weight(k):
         return copy(own_tile, wt.at[z, lq, :, lanes(rg)], s_w.at[0], r_w.at[0], z_peer(k))
 
     unrolled(1, NZ, lambda k: z_weight(k).start())
+    for c in local[1:]:
+        c.start()
     local[0].wait()
     arrived(wt.at[pl.ds(0, NZ - 1), lq, :, lanes(rg)], r_w.at[0])
 
@@ -271,7 +271,12 @@
     for k in range(1, NE):
         total = total + prec[k]
     zb[:, z] = total
-    unrolled(1, NZ, lambda k: copy(zb.at[:, z], zb.at[:, z], s_z.at[0], r_z.at[0], z_peer(k)).start())
+
+    def z_gram(h):
+        unrolled(1, NZ, lambda k: copy(zb.at[h, z], zb.at[h, z], s_z.at[h], r_z.at[h], z_peer(k)).start())
+
+    z_gram(0)
+    pl.when(z >= 8)(lambda: z_gram(1))
 
     rest_half.wait_recv()
 
@@ -287,24 +292,43 @@
         ).start())
 
     send_rest(0)
-    arrived(zb.at[:, pl.ds(0, NZ - 1)], r_z.at[0])
-
-    parts = (pl.ds(0, 1), pl.ds(1, 1), pl.ds(2, 1), pl.ds(3, 1), pl.ds(4, 2))
+    arrived(zb.at[0, pl.ds(0, NZ - 1)], r_z.at[0])
+    pl.when(z >= 8)(lambda: arrived(zb.at[1, pl.ds(0, 7)], r_z.at[1]))
+    pl.when(z < 8)(lambda: arrived(zb.at[1, pl.ds(0, 8)], r_z.at[1]))
+
     for p in range(4):
         gb[core, chip, p] = zb[0, pl.ds(((lq + 4 - p) % 4) * 4, 4)]
     gb[core, chip, 4:] = zb[1, 8:].reshape(2, 4, 8, 128)
 
+    def rows_of_chips(i):
+        return {2: ((0, 2), (3, 4)), 3: ((0, 3),), 4: ((2, 4),)}.get(i, ((0, 4),))
+
+    def has(i, run, otherwise=None):
+        if i in (0, 1, 5):
+            run()
+            return
+        yes = {2: lq != 2, 3: lq != 3, 4: lq >= 2}[i]
+        pl.when(yes)(run)
+        if otherwise is not None:
+            pl.when(jnp.logical_not(yes))(otherwise)
+
+    def senders(i):
+        return 4 * sum(b - a for a, b in rows_of_chips(i))
+
     def send_panels(i):
-        piece = gb.at[core, chip, parts[i]]
-        unrolled(1, NQ, lambda k: copy(piece, piece, s_a.at[i], r_a.at[i], chip_peer(k)).start())
+        piece = gb.at[core, chip, i]
+        has(i, lambda: unrolled(1, NQ, lambda k: copy(piece, piece, s_a.at[i], r_a.at[i], chip_peer(k)).start()))
 
     def pass_panels(i):
-        arrived(gb.at[core, pl.ds(0, NQ - 1), parts[i]], r_a.at[i])
-        piece = gb.at[core, :, parts[i]]
-        copy(piece, piece, s_b.at[i], r_b.at[i], mate).start()
+        n = senders(i)
+        has(i, lambda: arrived(gb.at[core, pl.ds(0, n - 1), i], r_a.at[i]), lambda: arrived(gb.at[core, pl.ds(0, n), i], r_a.at[i]))
+        for h, (a, b) in enumerate(rows_of_chips(i)):
+            piece = gb.at[core, pl.ds(4 * a, 4 * (b - a)), i]
+            copy(piece, piece, s_b.at[2 * i + h], r_b.at[2 * i + h], mate).start()
 
     def wait_panels(i):
-        arrived(gb.at[1 - core, :, parts[i]], r_b.at[i])
+        for h, (a, b) in enumerate(rows_of_chips(i)):
+            arrived(gb.at[1 - core, pl.ds(4 * a, 4 * (b - a)), i], r_b.at[2 * i + h])
 
     def panel(c, r0, r1):
         tiles = []
@@ -314,7 +338,7 @@
             tiles += [gb[i // 4, q * 4 + i % 4, slot, zz % 4] for i in range(8)]
         return jnp.concatenate(tiles, axis=0)
 
-    for i in range(5):
+    for i in (0, 1, 2, 3, 5, 4):
         send_panels(i)
 
     send_rest(1)
@@ -343,7 +367,7 @@
     def beside(c):
         work = []
         if c in (1, 2, 3):
-            work.append(lambda: pass_panels(c + 1))
+            work.append(lambda: pass_panels(c + 1 if c < 3 else 5))
         if c == REST_FROM:
             work.append(rest_ready)
             for k in range(c):
@@ -357,8 +381,12 @@
     def before(c):
         if c < 2:
             pass_panels(c)
-        if c in FIRST:
-            wait_panels(FIRST.index(c))
+        if c < 4:
+            wait_panels(c)
+        if c == 4:
+            pass_panels(4)
+            wait_panels(5)
+            wait_panels(4)
 
     cholesky(lambda c, r0, r1: panel(c, r0, r1) * scale, w, tts, hi_s, lo_s, p_hi, p_lo, dn, beside, before)
     rest_solve(N // B - 1)
@@ -371,13 +399,18 @@
     for y in range(4):
         arrived(wt.at[:, y, :, lanes(core * 4, 4)], s_m.at[y])
     arrived(prec.at[pl.ds(1, NE - 1)], s_g.at[0])
-    arrived(zb.at[:, pl.ds(0, NZ - 1)], s_z.at[0])
+    arrived(zb.at[0, pl.ds(0, NZ - 1)], s_z.at[0])
+    pl.when(z >= 8)(lambda: arrived(zb.at[1, pl.ds(0, NZ - 1)], s_z.at[1]))
     rest_half.wait_send()
     for h in range(2):
         arrived(rrecv.at[pl.ds(1, NQ - 1), :, columns[h]], s_r.at[h])
-    for i in range(5):
-        arrived(gb.at[core, pl.ds(0, NQ - 1), parts[i]], s_a.at[i])
-        arrived(gb.at[core, :, parts[i]], s_b.at[i])
+    def panels_sent(i):
+        has(i, lambda: arrived(gb.at[core, pl.ds(0, NQ - 1), i], s_a.at[i]))
+        for h, (a, b) in enumerate(rows_of_chips(i)):
+            arrived(gb.at[core, pl.ds(4 * a, 4 * (b - a)), i], s_b.at[2 * i + h])
+
+    for i in range(6):
+        panels_sent(i)
 
 
 def on_device(samples, counts, panel_weight, rest_weight):
@@ -385,7 +418,7 @@
     own, wide = panel_weight.shape[1], rest_weight.shape[1]
     share = wide // NE
     vmem, anywhere = pl.BlockSpec(memory_space=pltpu.VMEM), pl.BlockSpec(memory_space=pltpu.HBM)
-    counted = [1, 1, 1, 4, 4, 4, 1, 1, 1, 1, 5, 5, 5, 5, 2, 2, 1, 1]
+    counted = [1, 1, 1, 4, 4, 4, 1, 1, 2, 2, 6, 6, 12, 12, 2, 2, 1, 1]
     return pl.pallas_call(
         functools.partial(kernel, share, 1.0 / (rows * NE)),
         out_shape=(jax.ShapeDtypeStruct((own, N), F32), jax.ShapeDtypeStruct((share, N), F32)),

time: 110 us -> 106 us (0.964)
  Pallas kernels: 105 us -> 101 us
    pallas_call x1, Pallas kernels: 105 us -> 101 us  [on_device(): pl.pallas_call(functools.partial(kernel, share, 1.0 / (rows * NE)), out_s...]
where the time goes in v7:
time: 106 us
  Pallas kernels  101 us (95%)
  local copies, waits for them, and re-layouts  3.21 us (3%)
  between operations  1.28 us (1%)
    pallas_call x1, Pallas kernels, on_device(): pl.pallas_call(functools.partial(kernel, share, 1.0 / (rows * NE)), out_s...  101 us
    unnamed x2, local copies, waits for them, and re-layouts  3.21 us

profile of v7, /device:TPU:1, one launch (start us, length us, event | category | flops | bytes accessed | tf_op | source)
XLA Modules:
  0.0 105.7 jit_solution(11605567269586726519)
XLA Ops:
  1.3 101.2 %shard_map.59 = (f32[64,1024]{1,0:T(8,128)}, f32[22,1024]{1,0:T(8,128)}) custom-call(bf16[1024,1024]{1,0:T(8,128)(2,1)} %x_ref.1, s32[1]{0:T(128)S(6)} %copy.8.n_ref, bf16[64,1024]{1,0:T(8,128)(2,1)} %bitcast.3, bf16[704,1024]{1,0:T(8,128)(2,1)} %bitcast.2), custom_call_target="tpu_custom_call" | custom-call | flops 10737418240 | bytes 8388608 | tf_op jit(solution)/shard_map/pallas_call | solution.py:422
  102.5 1.7 %copy.9 = f32[64,1024]{1,0:T(8,128)} copy(f32[64,1024]{1,0:T(8,128)} %get-tuple-element.4) | data formatting | bytes 524288
  104.1 1.5 %copy.10 = f32[22,1024]{1,0:T(8,128)} copy(f32[22,1024]{1,0:T(8,128)} %get-tuple-element.5) | data formatting | bytes 180224

commit v8 on v7

--- a/solution.py
+++ b/solution.py
@@ -202,12 +202,22 @@
     local[0].wait()
     arrived(wt.at[pl.ds(0, NZ - 1), lq, :, lanes(rg)], r_w.at[0])
 
-    tile = wt.at[:, lq, :, lanes(rg)]
-    unrolled(1, NQ, lambda k: copy(tile, tile, s_p.at[0], r_p.at[lq], chip_peer(k)).start())
-
-    def pass_weight(y):
-        piece = wt.at[:, y, :, lanes(core * 4, 4)]
-        copy(piece, piece, s_m.at[y], r_m.at[y], mate).start()
+    x = chip % 4
+
+    def along_x(piece, send, recv):
+        unrolled(1, 4, lambda k: copy(piece, piece, send, recv, {"ex": (lq * 4 + (x + k) % 4) * 2 + core}).start())
+
+    def along_y(piece, send, recv):
+        unrolled(1, 4, lambda k: copy(piece, piece, send, recv, {"ex": (((lq + k) % 4) * 4 + x) * 2 + core}).start())
+
+    def row_tiles(y, first=core * 4, count=4):
+        return wt.at[0:8, y, :, lanes(first, count)]
+
+    def column_tiles(i, count=4):
+        return wt.at[8:16, pl.ds(0, count), :, lanes(i)]
+
+    along_x(row_tiles(lq, rg, 1), s_p.at[0], r_p.at[0])
+    along_y(wt.at[8:16, lq, :, lanes(rg)], s_p.at[1], r_p.at[1])
 
     for c in local[1:]:
         c.wait()
@@ -217,6 +227,10 @@
         xs[at, :] = jnp.where(live, xs[at, :].astype(F32), 0.0).astype(BF16)
 
     blocks(rows // 256, 256, mask)
+    arrived(row_tiles(lq, core * 4, 3), r_p.at[0])
+    along_y(row_tiles(lq), s_p.at[2], r_p.at[2 + lq])
+    arrived(column_tiles(rg, 3), r_p.at[1])
+    along_x(column_tiles(rg), s_p.at[3], r_p.at[6 + x])
 
     def select(at):
         c = (lax.broadcasted_iota(jnp.int32, (128, 1), 0) + at.start).astype(F32)
@@ -235,12 +249,15 @@
     blocks(NE * SEL // 256, 256, rest_features)
     pt[...] = jnp.maximum(dot_nt(pt[...], xs[...]), 0.0).astype(BF16)
 
-    for y in range(4):
-        pl.when(lq == y)(lambda: arrived(wt.at[:, y, :, lanes(core * 4, 3)], r_p.at[y]))
-        pl.when(lq != y)(lambda: arrived(wt.at[:, y, :, lanes(core * 4, 4)], r_p.at[y]))
-        pass_weight(y)
-    for y in range(4):
-        arrived(wt.at[:, y, :, lanes(4 - core * 4, 4)], r_m.at[y])
+    for i in range(4):
+        pl.when(lq != i)(lambda: arrived(row_tiles(i), r_p.at[2 + i]))
+        copy(row_tiles(i), row_tiles(i), s_m.at[i], r_m.at[i], mate).start()
+        there = column_tiles(core * 4 + i)
+        pl.when(x != i)(lambda: arrived(there, r_p.at[6 + i]))
+        copy(there, there, s_m.at[4 + i], r_m.at[4 + i], mate).start()
+    for i in range(4):
+        arrived(row_tiles(i, 4 - core * 4), r_m.at[i])
+        arrived(column_tiles(4 - core * 4 + i), r_m.at[4 + i])
 
     def panel_features(at):
         pf[at, :] = jnp.maximum(dot_nt(xs[at, :], wt[...].reshape(N, DIN)), 0.0).astype(BF16)
@@ -395,9 +412,13 @@
     panel_out[...] = jnp.where(below, hi_s[ours, :].astype(F32) + lo_s[ours, :].astype(F32), 0.0)
 
     arrived(wt.at[pl.ds(0, NZ - 1), lq, :, lanes(rg)], s_w.at[0])
-    arrived(wt.at[:, 0:3, :, lanes(0, 5)], s_p.at[0])
-    for y in range(4):
-        arrived(wt.at[:, y, :, lanes(core * 4, 4)], s_m.at[y])
+    arrived(row_tiles(0, 0, 3), s_p.at[0])
+    arrived(row_tiles(0, 0, 3), s_p.at[1])
+    arrived(wt.at[0:8, 0:3, :, lanes(0, 4)], s_p.at[2])
+    arrived(wt.at[8:16, 0:3, :, lanes(0, 4)], s_p.at[3])
+    for i in range(4):
+        arrived(row_tiles(i), s_m.at[i])
+        arrived(column_tiles(core * 4 + i), s_m.at[4 + i])
     arrived(prec.at[pl.ds(1, NE - 1)], s_g.at[0])
     arrived(zb.at[0, pl.ds(0, NZ - 1)], s_z.at[0])
     pl.when(z >= 8)(lambda: arrived(zb.at[1, pl.ds(0, NZ - 1)], s_z.at[1]))
@@ -418,7 +439,7 @@
     own, wide = panel_weight.shape[1], rest_weight.shape[1]
     share = wide // NE
     vmem, anywhere = pl.BlockSpec(memory_space=pltpu.VMEM), pl.BlockSpec(memory_space=pltpu.HBM)
-    counted = [1, 1, 1, 4, 4, 4, 1, 1, 2, 2, 6, 6, 12, 12, 2, 2, 1, 1]
+    counted = [1, 1, 4, 10, 8, 8, 1, 1, 2, 2, 6, 6, 12, 12, 2, 2, 1, 1]
     return pl.pallas_call(
         functools.partial(kernel, share, 1.0 / (rows * NE)),
         out_shape=(jax.ShapeDtypeStruct((own, N), F32), jax.ShapeDtypeStruct((share, N), F32)),

time: 106 us -> 104 us (0.981)
  Pallas kernels: 101 us -> 98.7 us
    pallas_call x1, Pallas kernels: 101 us -> 98.7 us  [on_device(): pl.pallas_call(functools.partial(kernel, share, 1.0 / (rows * NE)), out_s...]
where the time goes in v8:
time: 104 us; the launch traced here: 103 us
  Pallas kernels  98.7 us (95%)
  local copies, waits for them, and re-layouts  3.21 us (3%)
  between operations  1.28 us (1%)
    pallas_call x1, Pallas kernels, on_device(): pl.pallas_call(functools.partial(kernel, share, 1.0 / (rows * NE)), out_s...  98.7 us
    unnamed x2, local copies, waits for them, and re-layouts  3.21 us

profile of v8, /device:TPU:1, one launch (start us, length us, event | category | flops | bytes accessed | tf_op | source)
XLA Modules:
  0.0 103.2 jit_solution(17243993253299073559)
XLA Ops:
  1.3 98.7 %shard_map.59 = (f32[64,1024]{1,0:T(8,128)}, f32[22,1024]{1,0:T(8,128)}) custom-call(bf16[1024,1024]{1,0:T(8,128)(2,1)} %x_ref.1, s32[1]{0:T(128)S(6)} %copy.8.n_ref, bf16[64,1024]{1,0:T(8,128)(2,1)} %bitcast.3, bf16[704,1024]{1,0:T(8,128)(2,1)} %bitcast.2), custom_call_target="tpu_custom_call" | custom-call | flops 10737418240 | bytes 8388608 | tf_op jit(solution)/shard_map/pallas_call | solution.py:443
  100.0 1.7 %copy.9 = f32[64,1024]{1,0:T(8,128)} copy(f32[64,1024]{1,0:T(8,128)} %get-tuple-element.4) | data formatting | bytes 524288
  101.6 1.5 %copy.10 = f32[22,1024]{1,0:T(8,128)} copy(f32[22,1024]{1,0:T(8,128)} %get-tuple-element.5) | data formatting | bytes 180224
